TPU v7x, 256 devices: a whole 4x4x8 slice. The times are simulated.
256 devices in a mesh: pts: 64 (over x, z, core), head: 4 (over y).
Axes of the slice: x: 4, y: 4, z: 8, core: 2. Of those that a mesh axis runs over, the one named last changes fastest.
Arguments:
- feats: bfloat16 [65536, 512], P('pts'), may hold values from -6 to 6
- neighbours: int32 [65536, 27], P('pts'), may hold values from -1 to 65535, as said below
- rank: int32 [65536], P('pts'), may hold values from 0 to 65535, as said below
- conv_weight: bfloat16 [27, 512, 512], P(None, None, 'head'), may hold values from -0.0546875 to 0.0546875
- cpe_gain: float32 [512], replicated, may hold values from 0.1 to 1.9
- norm1_gain: float32 [512], replicated, may hold values from 0.1 to 1.9
- w_query: bfloat16 [512, 512], P(None, 'head'), may hold values from -0.27 to 0.27
- w_key: bfloat16 [512, 512], P(None, 'head'), may hold values from -9 to 9
- w_value: bfloat16 [512, 512], P(None, 'head'), may hold values from -0.25 to 0.25
- w_proj: bfloat16 [512, 512], replicated, may hold values from -0.25 to 0.25
- norm2_gain: float32 [512], replicated, may hold values from 0.1 to 1.9
- w_fc1: bfloat16 [512, 2048], replicated, may hold values from -0.25 to 0.25
- w_fc2: bfloat16 [2048, 512], replicated, may hold values from -0.125 to 0.125
Outputs:
- block_out: bfloat16 [65536, 512], P('pts')
Inputs may be any that keep to these rules, and one draw needn't show every extreme that they name: `rank`: A permutation of the points. The points that one device holds (rows of 1024) reach the position range of any one device ([d * 1024, (d + 1) * 1024)) at most 28 times, and exactly 28 times for some pairs of devices in every draw. `neighbours`: tap (27 - 1) // 2 is the point itself; any other entry is -1 or an index j with 0 < |j - i| <= 256 (taps below the middle point backwards, the others forwards); the distance 256 is reached in every draw.
All inputs are finite; a program needn't handle non-finite values.
Results may differ from a plain program's by a relative error of at most 0.013.
The roundings to bfloat16 on the way count: a program that leaves them out, or rounds other values in their place, can miss the bound.
Values may be sent and summed in bfloat16 or wider, within the bound.
A program may use at most 192 MiB of HBM per device.

v0:
```python
import jax
import jax.numpy as jnp
from jax import lax
from jax.sharding import PartitionSpec as P

HD = 16
PATCH = 1024


def extended(cells, sides, width):
    for axis, dim in sides:
        count = lax.axis_size(axis)
        ends = count - 1
        head = lax.slice_in_dim(cells, 0, width, axis=dim)
        tail = lax.slice_in_dim(cells, cells.shape[dim] - width, cells.shape[dim], axis=dim)
        cells = jnp.concatenate(
            [
                lax.ppermute(tail, axis, [(i, (i + 1) % count) for i in range(ends)]),
                cells,
                lax.ppermute(head, axis, [((i + 1) % count, i) for i in range(ends)]),
            ],
            axis=dim,
        )
    return cells


def layer_norm(values, gain):
    centre = values - jnp.mean(values, -1, keepdims=True)
    spread = jnp.mean(centre * centre, -1, keepdims=True)
    return centre * lax.rsqrt(spread + 1e-05) * gain


def patch_attention(queries, keys_all, values_all):
    scores = jnp.einsum(
        "qhd,khd->hqk", queries, keys_all, preferred_element_type=jnp.float32
    ) / jnp.sqrt(jnp.float32(HD))
    probs = jax.nn.softmax(scores, axis=-1).astype(jnp.bfloat16)
    attended = jnp.einsum("hqk,khd->qhd", probs, values_all, preferred_element_type=jnp.float32)
    return attended.astype(jnp.bfloat16)


def project_fold(w_proj, piece):
    return jnp.dot(piece, w_proj, preferred_element_type=jnp.float32)


def per_device(
    feats,
    neighbours,
    rank,
    conv_weight,
    cpe_gain,
    norm1_gain,
    w_query,
    w_key,
    w_value,
    w_proj,
    norm2_gain,
    w_fc1,
    w_fc2,
):
    points, width = feats.shape
    taps = neighbours.shape[1]
    reach = points // 4
    devices = lax.axis_size("pts")
    head_width = w_value.shape[1]
    heads_dev = head_width // HD
    range_start = lax.axis_index("pts") * points
    padded = extended(feats, (("pts", 0),), reach)
    padded = jnp.concatenate([padded, jnp.zeros((1, width), jnp.bfloat16)], 0)
    local_rows = jnp.where(neighbours < 0, points + 2 * reach, neighbours - range_start + reach)
    stacked = padded[local_rows].reshape(points, taps * width)
    conv_part = jnp.dot(
        stacked, conv_weight.reshape(taps * width, head_width), preferred_element_type=jnp.float32
    ).astype(jnp.bfloat16)
    conv_full = lax.all_gather(conv_part, "head", axis=1, tiled=True)
    h_one = feats.astype(jnp.float32) + layer_norm(conv_full.astype(jnp.float32), cpe_gain)
    normed = layer_norm(h_one, norm1_gain).astype(jnp.bfloat16)
    capacity = 7 * points // (4 * devices)
    target = rank // points
    position = rank % points
    one_hot = (target[:, None] == jnp.arange(devices, dtype=jnp.int32)[None, :]).astype(
        jnp.bfloat16
    )
    earlier = (jnp.arange(points)[:, None] > jnp.arange(points)[None, :]).astype(jnp.bfloat16)
    counts = jnp.dot(earlier, one_hot, preferred_element_type=jnp.float32)
    slot_of = jnp.sum(counts * one_hot, 1).astype(jnp.int32)
    bucket = target * capacity + slot_of
    spots_out = (
        jnp.full((devices * capacity,), -1, jnp.int32)
        .at[bucket]
        .set(position)
        .reshape(devices, capacity)
    )
    outgoing = (
        jnp.zeros((devices * capacity, width), jnp.bfloat16)
        .at[bucket]
        .set(normed)
        .reshape(devices, capacity, width)
    )
    arrived, spots_in = (
        lax.all_to_all(outgoing, "pts", split_axis=0, concat_axis=0, tiled=True),
        lax.all_to_all(spots_out, "pts", split_axis=0, concat_axis=0, tiled=True),
    )
    spots_in = spots_in.reshape(-1)
    flat = arrived.reshape(devices * capacity, arrived.shape[-1])
    chosen = jnp.where(spots_in < 0, points, spots_in)
    placed = jnp.zeros((points, flat.shape[1]), jnp.bfloat16).at[chosen].set(flat, mode="drop")
    queries = jnp.dot(placed, w_query, preferred_element_type=jnp.float32).astype(jnp.bfloat16)
    keys_all = jnp.dot(placed, w_key, preferred_element_type=jnp.float32).astype(jnp.bfloat16)
    values_all = jnp.dot(placed, w_value, preferred_element_type=jnp.float32).astype(jnp.bfloat16)
    patches = points // PATCH
    shaped = tuple(
        (a.reshape(patches, PATCH, heads_dev, HD) for a in (queries, keys_all, values_all))
    )
    attended = lax.map(lambda group: patch_attention(*group), shaped).reshape(points, head_width)
    merged_owner = project_fold(
        w_proj, lax.all_gather(attended, "head", axis=1, tiled=True)
    ).astype(jnp.bfloat16)
    chosen = jnp.where(spots_in < 0, 0, spots_in)
    rows_back = jnp.where(
        (spots_in >= 0)[:, None], merged_owner[chosen], jnp.zeros((), jnp.bfloat16)
    )
    returned = lax.all_to_all(
        rows_back.reshape(devices, capacity, merged_owner.shape[1]),
        "pts",
        split_axis=0,
        concat_axis=0,
        tiled=True,
    )
    merged = returned.reshape(devices * capacity, width)[bucket]
    h_two = h_one + merged.astype(jnp.float32)
    normed2 = layer_norm(h_two, norm2_gain).astype(jnp.bfloat16)
    hidden = jax.nn.gelu(
        jnp.dot(normed2, w_fc1, preferred_element_type=jnp.float32), approximate=False
    ).astype(jnp.bfloat16)
    return (h_two + jnp.dot(hidden, w_fc2, preferred_element_type=jnp.float32)).astype(jnp.bfloat16)


def solution(mesh):
    placed = (
        P("pts", None),
        P("pts", None),
        P("pts"),
        P(None, None, "head"),
        P(),
        P(),
        P(None, "head"),
        P(None, "head"),
        P(None, "head"),
        P(),
        P(),
        P(),
        P(),
    )
    return jax.shard_map(
        per_device, mesh=mesh, in_specs=placed, out_specs=P("pts", None), check_vma=False
    )
```

profile of v0, /device:TPU:1, one launch (start us, length us, event | category | flops | bytes accessed | tf_op | source)
XLA Modules:
  0.0 526.0 jit_solution(11231077981323863586)
XLA Ops:
  6.5 2.0 fusion.98
  8.5 4.9 collective-permute-start
  13.5 2.2 collective-permute-start.1
  15.7 1.6 compare_select_fusion
  17.3 1.9 copy.23
  19.2 2.0 reshape.144
  21.2 1.6 broadcast_clamp_fusion
  22.8 2.9 maximum_maximum_fusion
  25.7 121.9 %gather_fusion = bf16[27648,512]{1,0:T(8,128)(2,1)} fusion(bf16[1537,512]{1,0:T(8,128)(2,1)} %maximum_maximum_fusion, s32[27648]{0:T(1024)} %broadcast_clamp_fusion), kind=kCustom, calls=%fused_computation | custom fusion | bytes 56733696 | tf_op jit(solution)/shard_map/gather | solution.py:71
  147.6 37.3 %reshape.143 = bf16[1024,27,512]{2,1,0:T(8,128)(2,1)} reshape(bf16[27648,512]{1,0:T(8,128)(2,1)} %gather_fusion) | data formatting | bytes 56623104 | tf_op jit(solution)/shard_map/gather | solution.py:71
  184.9 49.1 %fusion.35 = bf16[1024,128]{1,0:T(8,128)(2,1)} fusion(bf16[27,512,128]{2,1,0:T(8,128)(2,1)S(1)} %copy-done, bf16[1024,27,512]{2,1,0:T(8,128)(2,1)} %reshape.143), kind=kOutput, calls=%fused_computation.59 | convolution fusion | flops 3624009728 | bytes 32112640 | tf_op jit(solution)/shard_map/dot_general | solution.py:72
  234.1 0.6 fusion.40
  234.7 4.3 scatter_custom_fusion
  239.0 0.7 all_to_all.12
  239.7 12.6 %all-to-all-start = ((s32[64,1,28]{2,1,0:T(1,128)}), s32[64,1,28]{2,1,0:T(1,128)S(1)}, u32[]{:S(2)}, u32[]{:S(2)}) async-start(s32[64,1,28]{2,1,0:T(1,128)} %bitcast.1), calls=%async_computation | async-start | bytes 65536 | tf_op jit(solution)/shard_map/all_to_all | solution.py:102
  252.3 12.9 %all-gather.3.cloned.1.call-done = bf16[1024,512]{1,0:T(8,128)(2,1)} async-done(((bf16[1024,128]{1,0:T(8,128)(2,1)}), bf16[1024,512]{1,0:T(8,128)(2,1)}) %all-gather.3.cloned.1.call-update) | async-done | bytes 1048592 | tf_op jit(solution)/shard_map/all_gather | solution.py:75
  265.2 1.5 convert_reduce_fusion
  266.8 1.7 fusion.27
  268.5 0.8 fusion.97
  269.3 0.9 multiply_reduce_fusion.2
  270.2 6.9 %scatter_custom_fusion.1 = bf16[1792,512]{1,0:T(8,128)(2,1)} fusion(s32[1024]{0:T(1024)S(1)} %get-tuple-element.22, f32[512]{0:T(512)S(1)} %copy-done.11, f32[1024]{0:T(1024)S(1)} %add_rsqrt_fusion.1, f32[1024]{0:T(1024)S(1)} %broadcast_multiply_fusion.1, bf16[]{:T(256)} %constant.48.clone.1, bf16[1024,512]{1,0:T(8,128)(2,1)S(1)} %copy-done.2, ...), kind=kCustom, calls=%fused_computation.63 | custom fusion | flops 5242880 | bytes 3952642 | tf_op jit(solution)/shard_map/scatter | solution.py:97
  277.1 3.7 reshape.138
  280.9 11.5 %all-to-all-start.1 = ((bf16[64,28,512]{2,1,0:T(8,128)(2,1)}), bf16[64,28,512]{2,1,0:T(8,128)(2,1)S(1)}, u32[]{:S(2)}, u32[]{:S(2)}) async-start(bf16[64,28,512]{2,1,0:T(8,128)(2,1)} %reshape.138), calls=%async_computation.1 | async-start | bytes 4194304 | tf_op jit(solution)/shard_map/all_to_all | solution.py:101
  292.4 0.5 broadcast.215
  293.0 0.7 reduce.7
  293.7 0.1 reshape.137
  293.9 49.8 %all-to-all-done.1 = bf16[64,28,512]{2,1,0:T(8,128)(2,1)S(1)} async-done(((bf16[64,28,512]{2,1,0:T(8,128)(2,1)}), bf16[64,28,512]{2,1,0:T(8,128)(2,1)S(1)}, u32[]{:S(2)}, u32[]{:S(2)}) %all-to-all-start.1) | async-done | bytes 1835040 | tf_op jit(solution)/shard_map/all_to_all | solution.py:101
  343.6 1.6 reshape.186
  345.2 11.1 %scatter_custom_fusion.2 = bf16[1024,512]{1,0:T(8,128)(2,1)S(1)} fusion(s32[1792]{0:T(1024)S(1)} %get-tuple-element.14, bf16[1792,512]{1,0:T(8,128)(2,1)} %reshape.186, bf16[]{:T(256)} %constant.48.clone.1), kind=kCustom, calls=%fused_computation.72 | custom fusion | bytes 1049088 | tf_op jit(solution)/shard_map/scatter | solution.py:107
  356.3 0.5 convolution_convert_fusion.2
  356.8 0.5 convolution_convert_fusion.1
  357.3 0.5 convolution_convert_fusion.3
  357.8 14.6 %fusion.99 = (f32[8,1024]{1,0:T(8,128)S(1)}, f32[8,1024,1024]{1,2,0:T(8,128)}) fusion(bf16[1024,8,16]{0,2,1:T(8,128)(2,1)S(1)} %bitcast.32, bf16[1024,8,16]{0,2,1:T(8,128)(2,1)S(1)} %bitcast.33), kind=kOutput, calls=%fused_computation.138 | convolution fusion | flops 293602304 | bytes 34111488 | tf_op jit(solution)/shard_map/while/body/eval_jaxpr/sub | solution.py:37
  372.4 12.6 %fusion.38 = bf16[8,16,1024]{2,1,0:T(8,128)(2,1)} fusion(bf16[1024,8,16]{0,2,1:T(8,128)(2,1)S(1)} %bitcast.31, f32[8,1024,1024]{1,2,0:T(8,128)} %get-tuple-element.28, f32[8,1024]{1,0:T(8,128)S(1)} %get-tuple-element.27), kind=kOutput, calls=%fused_computation.60 | convolution fusion | flops 285343744 | bytes 34111488 | tf_op jit(solution)/shard_map/while/body/eval_jaxpr/hqk,khd->qhd/dot_general | solution.py:38
  385.0 0.1 copy.26
  385.0 0.1 copy.27
  385.2 21.7 %all-gather.5.cloned.1.call-done = bf16[1024,512]{0,1:T(8,128)(2,1)} async-done(((bf16[1024,128]{0,1:T(8,128)(2,1)}), bf16[1024,512]{0,1:T(8,128)(2,1)}) %all-gather.5.cloned.1.call-update) | async-done | bytes 1048592 | tf_op jit(solution)/shard_map/all_gather | solution.py:117
  406.9 2.0 convolution_convert_fusion
  408.9 6.1 %gather_fusion.1 = bf16[1792,512]{1,0:T(8,128)(2,1)} fusion(bf16[1024,512]{1,0:T(8,128)(2,1)S(1)} %convolution_convert_fusion, s32[2048]{0:T(1024)S(1)} %pad_clamp_fusion), kind=kCustom, calls=%fused_computation.1 | custom fusion | bytes 3677184 | tf_op jit(solution)/shard_map/gather | solution.py:121
  415.0 2.4 gather.13
  417.4 0.5 broadcast_select_fusion
  417.9 62.7 %all_to_all.19 = bf16[64,28,512]{2,1,0:T(8,128)(2,1)} all-to-all(bf16[64,28,512]{2,1,0:T(8,128)(2,1)S(1)} %broadcast_select_fusion), channel_id=1, replica_groups=mesh['pts'=64,'head'=4] {'pts'}, dimensions={0} | all-to-all | bytes 3670016 | tf_op jit(solution)/shard_map/all_to_all | solution.py:123
  480.6 2.5 reshape.141
  483.0 5.1 gather_fusion.2
  488.1 2.6 fusion.52
  490.8 1.2 multiply_reduce_fusion.1
  491.9 0.6 add_rsqrt_fusion
  492.5 26.4 %add_convert_fusion = bf16[1024,512]{1,0:T(8,128)(2,1)} fusion(bf16[2048,512]{1,0:T(8,128)(2,1)} %param.25, bf16[512,2048]{1,0:T(8,128)(2,1)} %param.24, f32[512]{0:T(512)} %param.23, f32[1024]{0:T(1024)} %add_rsqrt_fusion, f32[1024]{0:T(1024)S(1)} %broadcast_multiply_fusion, bf16[1024,512]{1,0:T(8,128)(2,1)} %gather_fusion.2, f32[512]{0:T(512)S(1)} %copy-done.9, ...), kind=kOutput, calls=%fused_computation.46 | convolution fusion | flops 4442816512 | bytes 8409088 | tf_op jit(solution)/shard_map/dot_general | solution.py:136
  (44 shorter events, 0.3 us)
Async XLA Ops:
  6.5 178.4 %copy-start = (bf16[27,512,128]{2,1,0:T(8,128)(2,1)S(1)}, bf16[27,512,128]{2,1,0:T(8,128)(2,1)}, u32[]{:S(2)}) copy-start(bf16[27,512,128]{2,1,0:T(8,128)(2,1)} %param.16) | copy-start | bytes 10616836
  6.5 258.7 %all-gather.3.cloned.1.call-start = ((), (), s32[]{:S(2)}) async-start(), calls=%async_computation.3 | async-start | bytes 1310720 | tf_op jit(solution)/shard_map/all_gather | solution.py:75
  8.5 14.3 %collective-permute-start = (bf16[256,512]{1,0:T(8,128)(2,1)}, bf16[256,512]{1,0:T(8,128)(2,1)}, u32[]{:S(2)}, u32[]{:S(2)}) collective-permute-start(bf16[256,512]{1,0:T(8,128)(2,1)} %get-tuple-element.24), channel_id=1, source_target_pairs={{0,4},{4,8},{8,12},{12,16},{16,20},{20,24},{24,28},{28,32},{32,36}... | collective-permute-start | bytes 786440 | tf_op jit(solution)/shard_map/ppermute | solution.py:18
  13.5 9.3 %collective-permute-start.1 = (bf16[256,512]{1,0:T(8,128)(2,1)}, bf16[256,512]{1,0:T(8,128)(2,1)}, u32[]{:S(2)}, u32[]{:S(2)}) collective-permute-start(bf16[256,512]{1,0:T(8,128)(2,1)} %get-tuple-element.25), channel_id=1, source_target_pairs={{4,0},{8,4},{12,8},{16,12},{20,16},{24,20},{28,24},{32,28},{36,32}... | collective-permute-start | bytes 786440 | tf_op jit(solution)/shard_map/ppermute | solution.py:20
  184.9 49.1 %copy-start.10 = (s32[1024]{0:T(1024)S(1)}, s32[1024]{0:T(1024)}, u32[]{:S(2)}) copy-start(s32[1024]{0:T(1024)} %param.15) | copy-start | bytes 12292
  234.0 34.5 %copy-start.3 = (bf16[1024,512]{1,0:T(8,128)(2,1)S(1)}, bf16[1024,512]{1,0:T(8,128)(2,1)}, u32[]{:S(2)}) copy-start(bf16[1024,512]{1,0:T(8,128)(2,1)} %param.13) | copy-start | bytes 3145732
  234.0 34.5 %copy-start.9 = (f32[512]{0:T(512)S(1)}, f32[512]{0:T(512)}, u32[]{:S(2)}) copy-start(f32[512]{0:T(512)} %param.17) | copy-start | bytes 6148
  239.7 41.1 %all-to-all-start = ((s32[64,1,28]{2,1,0:T(1,128)}), s32[64,1,28]{2,1,0:T(1,128)S(1)}, u32[]{:S(2)}, u32[]{:S(2)}) async-start(s32[64,1,28]{2,1,0:T(1,128)} %bitcast.1), calls=%async_computation | async-start | bytes 65536 | tf_op jit(solution)/shard_map/all_to_all | solution.py:102
  265.2 3.3 copy-start.2
  268.5 1.7 copy-start.11
  280.9 62.8 %all-to-all-start.1 = ((bf16[64,28,512]{2,1,0:T(8,128)(2,1)}), bf16[64,28,512]{2,1,0:T(8,128)(2,1)S(1)}, u32[]{:S(2)}, u32[]{:S(2)}) async-start(bf16[64,28,512]{2,1,0:T(8,128)(2,1)} %reshape.138), calls=%async_computation.1 | async-start | bytes 4194304 | tf_op jit(solution)/shard_map/all_to_all | solution.py:101
  292.4 114.5 %all-gather.5.cloned.1.call-start = ((), (), s32[]{:S(2)}) async-start(), calls=%async_computation.4 | async-start | bytes 1310720 | tf_op jit(solution)/shard_map/all_gather | solution.py:117
  293.9 62.5 %copy-start.6 = (bf16[512,128]{1,0:T(8,128)(2,1)S(1)}, bf16[512,128]{1,0:T(8,128)(2,1)}, u32[]{:S(2)}) copy-start(bf16[512,128]{1,0:T(8,128)(2,1)} %param.19) | copy-start | bytes 393220
  345.2 11.6 %copy-start.7 = (bf16[512,128]{1,0:T(8,128)(2,1)S(1)}, bf16[512,128]{1,0:T(8,128)(2,1)}, u32[]{:S(2)}) copy-start(bf16[512,128]{1,0:T(8,128)(2,1)} %param.20) | copy-start | bytes 393220
  345.2 12.1 %copy-start.8 = (bf16[512,128]{1,0:T(8,128)(2,1)S(1)}, bf16[512,128]{1,0:T(8,128)(2,1)}, u32[]{:S(2)}) copy-start(bf16[512,128]{1,0:T(8,128)(2,1)} %param.21) | copy-start | bytes 393220
  372.4 34.5 %copy-start.12 = (bf16[512,512]{1,0:T(8,128)(2,1)S(1)}, bf16[512,512]{1,0:T(8,128)(2,1)}, u32[]{:S(2)}) copy-start(bf16[512,512]{1,0:T(8,128)(2,1)} %param.22) | copy-start | bytes 1572868
  488.1 2.7 copy-start.4
  488.1 2.7 copy-start.5
  492.5 26.4 %copy-start.1 = (bf16[27,512,128]{2,1,0:T(8,128)(2,1)S(1)}, bf16[27,512,128]{2,1,0:T(8,128)(2,1)}, u32[]{:S(2)}) copy-start(bf16[27,512,128]{2,1,0:T(8,128)(2,1)} %param.16) | copy-start | bytes 10616836
Sparse Core Ops, SparseCore 0:
  234.2 31.0 all-gather.2
  385.1 21.7 all-gather.4
where the time goes:
time: 532 us; the launch traced here: 526 us
  local copies, waits for them, and re-layouts  203 us (38%)
  matrix products  107 us (20%)
  waiting for transfers between devices  84.4 us (16%)
  blocking collectives  62.7 us (12%)
  starting transfers between devices  31.3 us (6%)
  other arithmetic  23.5 us (4%)
  between operations  14 us (3%)
    gather x2, local copies, waits for them, and re-layouts, per_device(): stacked = padded[local_rows].reshape(points, taps * width)  159 us
    all_to_all x1, blocking collectives, per_device(): lax.all_to_all(rows_back.reshape(devices, capacity, merged_owner.shape[1]...  62.7 us
    all_to_all x1, waiting for transfers between devices, per_device(): lax.all_to_all(outgoing, 'pts', split_axis=0, concat_axis=0, tiled=True)  49.8 us
    dot_general x1, matrix products, per_device(): jnp.dot(stacked, conv_weight.reshape(taps * width, head_width), preferred...  49.1 us
    dot_general x1, matrix products, per_device(): jnp.dot(hidden, w_fc2, preferred_element_type=jnp.float32)  26.4 us
    all_gather x1, waiting for transfers between devices, per_device(): lax.all_gather(attended, 'head', axis=1, tiled=True)  21.7 us
    sub x1, matrix products, patch_attention(): probs = jax.nn.softmax(scores, axis=-1).astype(jnp.bfloat16)  14.6 us
    all_gather x1, waiting for transfers between devices, per_device(): conv_full = lax.all_gather(conv_part, 'head', axis=1, tiled=True)  12.9 us
  transfers between devices with their start and end apart: 6, of which 3 were waited for; matrix products, arithmetic and copies ran while one was open for 6% of the time, Pallas kernels for 0%

commit v1 on v0

v1 whole, which is shorter than its diff:
```python
import functools

import jax
import jax.numpy as jnp
import numpy as np
from jax import lax
from jax.experimental import pallas as pl
from jax.experimental.pallas import tpu as pltpu
from jax.sharding import PartitionSpec as P

HD = 16
PTS = 1024
REACH = 256
TAPS = 27
MID = 13
C = 512
W = 128
DEVS = 64
SLOTS = 32
ROWS = DEVS * SLOTS
BLK = 256
BF = jnp.bfloat16
F32 = jnp.float32
I32 = jnp.int32
VMEM = pltpu.MemorySpace.VMEM


def iota(shape, dim):
    return lax.broadcasted_iota(I32, shape, dim)


def dot(a, b):
    return jnp.dot(a, b, preferred_element_type=F32)


def dot_nt(a, b):
    return lax.dot_general(a, b, (((1,), (1,)), ((), ())), preferred_element_type=F32)


def hot(mask):
    return jnp.where(mask, 1.0, 0.0).astype(BF)


def conv_project(ext_ref, w_ref, yb_ref, yf_ref):
    for start, first, count, y_ref in ((0, 0, MID + 1, yb_ref), (REACH, MID + 1, MID, yf_ref)):
        rows = ext_ref.at[pl.ds(start, PTS + REACH)]

        @pl.loop(0, count // 2)
        def _(j):
            pair = jnp.concatenate([w_ref[first + 2 * j], w_ref[first + 2 * j + 1]], 1)
            y = dot(rows[...], pair).astype(BF)
            y_ref[2 * j] = y[:, :W]
            y_ref[2 * j + 1] = y[:, W:]

        if count % 2:
            y_ref[count - 1] = dot(rows[...], w_ref[first + count - 1]).astype(BF)


def conv_select(a, base, nbr_ref, yb_ref, yf_ref):
    start = pl.multiple_of(a * BLK, BLK)
    nbr = nbr_ref[pl.ds(start, BLK), :]
    at = nbr - (base + start)
    at = jnp.where(nbr < 0, -4096, at)
    window = iota((BLK, 2 * BLK), 1)
    acc = yb_ref[MID, pl.ds(start + REACH, BLK), :].astype(F32)
    for t in range(TAPS):
        if t == MID:
            continue
        if t < MID:
            sel = hot(window == at[:, t : t + 1] + REACH)
            acc += dot(sel, yb_ref[t, pl.ds(start, 2 * BLK), :])
        else:
            sel = hot(window == at[:, t : t + 1])
            acc += dot(sel, yf_ref[t - MID - 1, pl.ds(start, 2 * BLK), :])
    return acc


def conv_kernel(base_ref, ext_ref, nbr_ref, w_ref, out_ref, yb_ref, yf_ref):
    conv_project(ext_ref, w_ref, yb_ref, yf_ref)

    @pl.loop(0, PTS // BLK)
    def _(a):
        acc = conv_select(a, base_ref[0], nbr_ref, yb_ref, yf_ref)
        out_ref[pl.ds(pl.multiple_of(a * BLK, BLK), BLK), :] = acc.astype(BF)


def norm_slices(parts, gain_ref):
    mean = sum(jnp.sum(p, 1, keepdims=True) for p in parts) * (1.0 / C)
    centre = [p - mean for p in parts]
    spread = sum(jnp.sum(c * c, 1, keepdims=True) for c in centre) * (1.0 / C)
    scale = lax.rsqrt(spread + 1e-05)
    return [c * scale * gain_ref[:, W * k : W * k + W] for k, c in enumerate(centre)]


def mid_block(a, conv_ref, feats_ref, cpe_ref, n1_ref, h1_ref, normed_ref):
    rows = pl.ds(pl.multiple_of(a * BLK, BLK), BLK)
    conv = [conv_ref[k, rows, :].astype(F32) for k in range(4)]
    normed = norm_slices(conv, cpe_ref)
    h1 = [feats_ref[rows, W * k : W * k + W].astype(F32) + normed[k] for k in range(4)]
    for k, part in enumerate(norm_slices(h1, n1_ref)):
        h1_ref[rows, W * k : W * k + W] = h1[k]
        normed_ref[k, rows, :] = part.astype(BF)


def bucket_of_row(rank_row):
    target = rank_row // PTS
    ohT = hot(iota((DEVS, PTS), 0) == target)
    upper = hot(iota((PTS, PTS), 0) < iota((PTS, PTS), 1))
    counts = dot(ohT, upper)
    slot = jnp.sum(counts * ohT.astype(F32), 0, keepdims=True).astype(I32)
    code = rank_row % PTS + 1
    by_slot = hot(iota((W, PTS), 0) == slot)
    ohf = ohT.astype(F32)
    high = dot_nt((ohf * (code // 32).astype(F32)).astype(BF), by_slot)
    low = dot_nt((ohf * (code % 32).astype(F32)).astype(BF), by_slot)
    return target * SLOTS + slot, jnp.concatenate([high, low], 0).astype(BF)


def bucket_of_column(rank_col):
    target = rank_col // PTS
    oh = hot(iota((PTS, DEVS), 1) == target)
    lower = hot(iota((PTS, PTS), 1) < iota((PTS, PTS), 0))
    counts = dot(lower, oh)
    slot = jnp.sum(counts * oh.astype(F32), 1, keepdims=True).astype(I32)
    return target * SLOTS + slot


def pack_rows(bucket_row, positions, own, out_ref):
    @pl.loop(0, ROWS // BLK)
    def _(b):
        start = pl.multiple_of(b * BLK, BLK)
        sel = hot(iota((BLK, PTS), 0) + start == bucket_row)
        r = iota((BLK, W), 0) + start
        c = iota((BLK, W), 1)
        s = r % SLOTS
        d = r // SLOTS
        place = hot(((s == 28) & (c == d)) | ((s == 29) & (c == d + DEVS)))
        out_ref[pl.ds(start, BLK), :] = (dot(sel, own) + dot(place, positions)).astype(BF)


def digits_of(arrived):
    r = iota((DEVS, ROWS), 1)
    q = iota((DEVS, ROWS), 0)
    high = dot(hot(r == q * SLOTS + 28), arrived).astype(BF)
    low = dot(hot(r == q * SLOTS + 29), arrived).astype(BF)
    return high, low


def spots_row(high, low):
    pick = hot(iota((W, ROWS), 0) == iota((W, ROWS), 1) % SLOTS)
    full = dot(high, pick) * 32.0 + dot(low, pick) - 1.0
    mine = iota((DEVS, ROWS), 0) == iota((DEVS, ROWS), 1) // SLOTS
    return jnp.sum(jnp.where(mine, full, 0.0), 0, keepdims=True).astype(I32)


def spots_column(high, low, start, count):
    r = iota((count, DEVS), 0) + start
    pick = hot(iota((count, DEVS), 1) == r // SLOTS)
    full = dot(pick, high) * 32.0 + dot(pick, low) - 1.0
    mine = iota((count, W), 1) == (iota((count, W), 0) + start) % SLOTS
    return jnp.sum(jnp.where(mine, full, 0.0), 1, keepdims=True).astype(I32)


def place_rows(spots, arrived_ref, out_ref):
    @pl.loop(0, PTS // BLK)
    def _(b):
        start = pl.multiple_of(b * BLK, BLK)
        sel = hot(iota((BLK, ROWS), 0) + start == spots)
        out_ref[pl.ds(start, BLK), :] = dot(sel, arrived_ref[...]).astype(BF)


def unplace_rows(high, low, own_ref, out_ref):
    @pl.loop(0, ROWS // BLK)
    def _(b):
        start = pl.multiple_of(b * BLK, BLK)
        spots = spots_column(high, low, start, BLK)
        sel = hot(iota((BLK, PTS), 1) == spots)
        out_ref[pl.ds(start, BLK), :] = dot(sel, own_ref[...]).astype(BF)


def unpack_rows(bucket_col_ref, returned_ref, out_ref):
    @pl.loop(0, PTS // BLK)
    def _(b):
        start = pl.multiple_of(b * BLK, BLK)
        bucket = bucket_col_ref[pl.ds(start, BLK), :]
        sel = hot(iota((BLK, ROWS), 1) == bucket)
        out_ref[pl.ds(start, BLK), :] = dot(sel, returned_ref[...]).astype(BF)


def mid_kernel(conv_ref, feats_ref, rank_ref, cpe_ref, n1_ref, h1_ref, out_ref, normed_ref):
    @pl.loop(0, PTS // BLK)
    def _(a):
        mid_block(a, conv_ref, feats_ref, cpe_ref, n1_ref, h1_ref, normed_ref)

    bucket, positions = bucket_of_row(rank_ref[...])
    pack_rows(bucket, positions, normed_ref[lax.axis_index("head")], out_ref)


def place_kernel(arrived_ref, out_ref):
    high, low = digits_of(arrived_ref[...])
    place_rows(spots_row(high, low), arrived_ref, out_ref)


def attend(x_ref, wq_ref, wk_ref, wv_ref, qq_ref, k_ref, v_ref, acc_ref, att_ref):
    def project(w_ref):
        return sum(dot(x_ref[k], w_ref[W * k : W * k + W, :]) for k in range(4)).astype(BF)

    scaled = project(wq_ref).astype(F32) * np.float32(np.log2(np.e) / 4.0)
    high = scaled.astype(BF)
    qq_ref[:, :W] = high
    qq_ref[:, W:] = (scaled - high.astype(F32)).astype(BF)
    k_ref[...] = project(wk_ref)
    v_ref[...] = project(wv_ref)
    acc_ref[...] = jnp.zeros_like(acc_ref)
    lane = iota((PTS, W), 1) // HD

    @pl.loop(0, W // HD)
    def _(h):
        own = lane == h
        zero = jnp.zeros((PTS, W), BF)
        keys = jnp.where(own, k_ref[...], zero)
        keys = jnp.concatenate([keys, keys], 1)
        values = jnp.concatenate([jnp.where(own, v_ref[...], zero), hot(own)], 1)
        for b in range(PTS // BLK):
            rows = slice(b * BLK, b * BLK + BLK)
            scores = dot_nt(qq_ref[rows, :], keys)
            top = jnp.max(scores, 1, keepdims=True)
            probs = jnp.exp2(scores - top).astype(BF)
            acc_ref[rows, :] += dot(probs, values)

    att_ref[...] = (acc_ref[:, :W] / acc_ref[:, W:]).astype(BF)


def attend_kernel(
    x_ref, arrived_ref, wq_ref, wk_ref, wv_ref, out_ref, qq_ref, k_ref, v_ref, acc_ref, att_ref
):
    attend(x_ref, wq_ref, wk_ref, wv_ref, qq_ref, k_ref, v_ref, acc_ref, att_ref)
    high, low = digits_of(arrived_ref[...])
    unplace_rows(high, low, att_ref, out_ref)


def unpack_kernel(returned_ref, rank_ref, out_ref, bucket_ref):
    bucket_ref[...] = bucket_of_column(rank_ref[...])
    unpack_rows(bucket_ref, returned_ref, out_ref)


def mlp_block(a, att_ref, h1_ref, wp_ref, n2_ref, f1_ref, f2_ref, out_ref):
    rows = pl.ds(pl.multiple_of(a * BLK, BLK), BLK)
    merged = sum(dot(att_ref[k, rows, :], wp_ref[W * k : W * k + W, :]) for k in range(4))
    h2 = h1_ref[rows, :] + merged.astype(BF).astype(F32)
    parts = norm_slices([h2[:, W * k : W * k + W] for k in range(4)], n2_ref)
    normed = jnp.concatenate([p.astype(BF) for p in parts], 1)
    total = h2
    for j in range(4):
        cols = slice(C * j, C * j + C)
        x = dot(normed, f1_ref[:, cols])
        hidden = (0.5 * x * (1.0 + lax.erf(x * np.float32(np.sqrt(0.5))))).astype(BF)
        total += dot(hidden, f2_ref[cols, :])
    out_ref[rows, :] = total.astype(BF)


def mlp_kernel(att_ref, h1_ref, wp_ref, n2_ref, f1_ref, f2_ref, out_ref):
    @pl.loop(0, PTS // BLK)
    def _(a):
        mlp_block(a, att_ref, h1_ref, wp_ref, n2_ref, f1_ref, f2_ref, out_ref)


def call(kernel, outs, scratch, *args, smem=0):
    spaces = [pltpu.MemorySpace.SMEM] * smem + [VMEM] * (len(args) - smem)
    many = isinstance(outs, (list, tuple))
    return pl.pallas_call(
        kernel,
        out_shape=outs,
        in_specs=[pl.BlockSpec(memory_space=s) for s in spaces],
        out_specs=[pl.BlockSpec(memory_space=VMEM)] * len(outs)
        if many
        else pl.BlockSpec(memory_space=VMEM),
        scratch_shapes=scratch,
        compiler_params=pltpu.CompilerParams(vmem_limit_bytes=48 * 2**20),
    )(*args)


def shape(dims, dtype=BF):
    return jax.ShapeDtypeStruct(dims, dtype)


def conv_local(base, ext, neighbours, conv_weight):
    return call(
        conv_kernel,
        shape((PTS, W)),
        [pltpu.VMEM((MID + 1, PTS + REACH, W), BF), pltpu.VMEM((MID, PTS + REACH, W), BF)],
        base,
        ext,
        neighbours,
        conv_weight,
        smem=1,
    )


def attend_local(x, arrived, w_query, w_key, w_value):
    return call(
        attend_kernel,
        shape((ROWS, W)),
        [
            pltpu.VMEM((PTS, 2 * W), BF),
            pltpu.VMEM((PTS, W), BF),
            pltpu.VMEM((PTS, W), BF),
            pltpu.VMEM((PTS, 2 * W), F32),
            pltpu.VMEM((PTS, W), BF),
        ],
        x,
        arrived,
        w_query,
        w_key,
        w_value,
    )


def exchange(rows):
    blocks = rows.reshape(DEVS, SLOTS, W)
    return lax.all_to_all(blocks, "pts", split_axis=0, concat_axis=0, tiled=True).reshape(ROWS, W)


def per_device(
    feats,
    neighbours,
    rank,
    conv_weight,
    cpe_gain,
    norm1_gain,
    w_query,
    w_key,
    w_value,
    w_proj,
    norm2_gain,
    w_fc1,
    w_fc2,
):
    count = lax.axis_size("pts")
    me = lax.axis_index("pts")
    up = [(i, i + 1) for i in range(count - 1)]
    down = [(i + 1, i) for i in range(count - 1)]
    ext = jnp.concatenate(
        [
            lax.ppermute(feats[PTS - REACH :], "pts", up),
            feats,
            lax.ppermute(feats[:REACH], "pts", down),
        ],
        0,
    )
    base = (me * PTS).astype(I32).reshape(1)
    conv = conv_local(base, ext, neighbours, conv_weight)
    conv_full = lax.all_gather(conv, "head", axis=0, tiled=False)
    rank_row, rank_col = rank.reshape(1, PTS), rank.reshape(PTS, 1)
    h_one, outgoing = call(
        mid_kernel,
        [shape((PTS, C), F32), shape((ROWS, W))],
        [pltpu.VMEM((4, PTS, W), BF)],
        conv_full,
        feats,
        rank_row,
        cpe_gain.reshape(1, C),
        norm1_gain.reshape(1, C),
    )
    arrived = exchange(outgoing)
    placed = call(place_kernel, shape((PTS, W)), [], arrived)
    placed_full = lax.all_gather(placed, "head", axis=0, tiled=False)
    rows_back = attend_local(placed_full, arrived, w_query, w_key, w_value)
    returned = exchange(rows_back)
    attended = call(
        unpack_kernel, shape((PTS, W)), [pltpu.VMEM((PTS, 1), I32)], returned, rank_col
    )
    attended_full = lax.all_gather(attended, "head", axis=0, tiled=False)
    return call(
        mlp_kernel,
        shape((PTS, C)),
        [],
        attended_full,
        h_one,
        w_proj,
        norm2_gain.reshape(1, C),
        w_fc1,
        w_fc2,
    )


def solution(mesh):
    placed = (
        P("pts", None),
        P("pts", None),
        P("pts"),
        P(None, None, "head"),
        P(),
        P(),
        P(None, "head"),
        P(None, "head"),
        P(None, "head"),
        P(),
        P(),
        P(),
        P(),
    )
    return jax.shard_map(
        per_device, mesh=mesh, in_specs=placed, out_specs=P("pts", None), check_vma=False
    )
```

time: 532 us -> 228 us (0.43)
  local copies, waits for them, and re-layouts: 203 us -> 12.2 us
  matrix products: 107 us -> 0 us
  Pallas kernels: 0 us -> 61 us
  blocking collectives: 62.7 us -> 28.7 us
  other arithmetic: 23.5 us -> 0.1 us
  starting transfers between devices: 31.3 us -> 18.8 us
  waiting for transfers between devices: 84.4 us -> 93.1 us
    gather x5 -> x0, local copies, waits for them, and re-layouts: 173 us -> none  [the longest x2 159 us: per_device(): stacked = padded[local_rows].reshape(points, taps * width)]
    dot_general x8 -> x0, matrix products: 92 us -> none  [the longest x1 49.1 us: per_device(): jnp.dot(stacked, conv_weight.reshape(taps * width, head_width), preferred...]
    pallas_call x0 -> x6, Pallas kernels: none -> 61 us  [call(): pl.pallas_call(kernel, out_shape=outs, in_specs=[pl.BlockSpec(memory_spac...]
    all_gather x2 -> x3, waiting for transfers between devices: 34.6 us -> 71.5 us  [the longest x1 28.1 us: per_device(): conv_full = lax.all_gather(conv, 'head', axis=0, tiled=False)]
    all_to_all x1, blocking collectives: 62.7 us -> 28.7 us  [exchange(): lax.all_to_all(blocks, 'pts', split_axis=0, concat_axis=0, tiled=True)]
    all_to_all x2 -> x1, waiting for transfers between devices: 49.8 us -> 16.9 us  [exchange(): lax.all_to_all(blocks, 'pts', split_axis=0, concat_axis=0, tiled=True)]
    scatter x2 -> x0, local copies, waits for them, and re-layouts: 15.4 us -> none  [the longest x1 11.1 us: per_device(): jnp.zeros((points, flat.shape[1]), jnp.bfloat16).at[chosen]]
    sub x1 -> x0, matrix products: 14.6 us -> none  [patch_attention(): probs = jax.nn.softmax(scores, axis=-1).astype(jnp.bfloat16)]
  transfers between devices with their start and end apart: 6 -> 6, of which waited for: 3 -> 6; matrix products, arithmetic and copies ran while one was open for 6% -> 1% of each run, Pallas kernels for 0% -> 0%
where the time goes in v1:
time: 228 us; the launch traced here: 227 us
  waiting for transfers between devices  93.1 us (41%)
  Pallas kernels  61 us (27%)
  blocking collectives  28.7 us (13%)
  starting transfers between devices  18.8 us (8%)
  between operations  13.2 us (6%)
  local copies, waits for them, and re-layouts  12.2 us (5%)
    pallas_call x6, Pallas kernels, call(): pl.pallas_call(kernel, out_shape=outs, in_specs=[pl.BlockSpec(memory_spac...  61 us
    all_to_all x1, blocking collectives, exchange(): lax.all_to_all(blocks, 'pts', split_axis=0, concat_axis=0, tiled=True)  28.7 us
    all_gather x1, waiting for transfers between devices, per_device(): conv_full = lax.all_gather(conv, 'head', axis=0, tiled=False)  28.1 us
    all_gather x1, waiting for transfers between devices, per_device(): attended_full = lax.all_gather(attended, 'head', axis=0, tiled=False)  21.8 us
    all_gather x1, waiting for transfers between devices, per_device(): placed_full = lax.all_gather(placed, 'head', axis=0, tiled=False)  21.7 us
    all_to_all x1, waiting for transfers between devices, exchange(): lax.all_to_all(blocks, 'pts', split_axis=0, concat_axis=0, tiled=True)  16.9 us
    all_to_all x1, starting transfers between devices, exchange(): lax.all_to_all(blocks, 'pts', split_axis=0, concat_axis=0, tiled=True)  11.7 us
    unnamed x33, local copies, waits for them, and re-layouts  10.8 us
  transfers between devices with their start and end apart: 6, of which 6 were waited for; matrix products, arithmetic and copies ran while one was open for 1% of the time, Pallas kernels for 0%

profile of v1, /device:TPU:1, one launch (start us, length us, event | category | flops | bytes accessed | tf_op | source)
XLA Modules:
  0.0 227.1 jit_solution(13618106660554218574)
XLA Ops:
  6.5 0.0 copy-start
  6.5 0.0 all-gather.7.cloned.1.call-start
  6.5 1.2 fusion
  7.7 4.9 %collective-permute-start = (bf16[256,512]{1,0:T(8,128)(2,1)S(1)}, bf16[256,512]{1,0:T(8,128)(2,1)S(1)}, u32[]{:S(2)}, u32[]{:S(2)}) collective-permute-start(bf16[256,512]{1,0:T(8,128)(2,1)S(1)} %get-tuple-element.9), channel_id=1, source_target_pairs={{0,4},{4,8},{8,12},{12,16},{16,20},{20,24},{24,28},{28,32},{32,36}... | collective-permute-start | bytes 786440 | tf_op jit(solution)/shard_map/ppermute | solution.py:345
  12.6 1.9 collective-permute-start.1
  14.6 1.1 copy.15.nbr_ref
  15.7 0.2 collective-permute-done
  15.9 4.4 %collective-permute-done.1 = bf16[256,512]{1,0:T(8,128)(2,1)S(1)} collective-permute-done((bf16[256,512]{1,0:T(8,128)(2,1)S(1)}, bf16[256,512]{1,0:T(8,128)(2,1)S(1)}, u32[]{:S(2)}, u32[]{:S(2)}) %collective-permute-start.1) | collective-permute-done | bytes 262176 | tf_op jit(solution)/shard_map/ppermute | solution.py:347
  20.3 0.0 copy-done
  20.3 0.1 pad_maximum_fusion.ext_ref
  20.4 0.0 copy-start.1
  20.5 2.0 copy-done.1
  22.4 0.0 copy-start.12
  22.4 0.0 copy-start.14
  22.4 0.0 copy-start.15
  22.4 15.8 %shard_map.127 = bf16[1024,128]{1,0:T(8,128)(2,1)} custom-call(s32[1]{0:T(128)} %bitcast.base_ref, bf16[1536,512]{1,0:T(8,128)(2,1)S(1)} %pad_maximum_fusion.ext_ref, s32[1024,27]{1,0:T(8,128)S(1)} %copy.15.nbr_ref, bf16[27,512,128]{2,1,0:T(8,128)(2,1)S(1)} %copy-done.1), custom_call_target="tpu_custom_call" | custom-call | tf_op jit(solution)/shard_map/pallas_call | solution.py:271
  38.2 0.0 all-gather.7.cloned.1.call-update
  38.2 0.0 all-gather.9.cloned.1.call-start
  38.3 28.1 %all-gather.7.cloned.1.call-done = bf16[4096,128]{1,0:T(8,128)(2,1)} async-done(((bf16[1024,128]{1,0:T(8,128)(2,1)}), bf16[4096,128]{1,0:T(8,128)(2,1)}) %all-gather.7.cloned.1.call-update) | async-done | bytes 1048592 | tf_op jit(solution)/shard_map/all_gather | solution.py:353
  66.3 0.0 copy-done.12
  66.3 0.0 copy-done.14
  66.3 0.0 copy-done.15
  66.3 1.2 copy-done.6
  67.6 7.2 %shard_map.128 = (f32[1024,512]{1,0:T(8,128)S(1)}, bf16[2048,128]{1,0:T(8,128)(2,1)S(1)}) custom-call(bf16[4,1024,128]{2,1,0:T(8,128)(2,1)S(1)} %bitcast.17, bf16[1024,512]{1,0:T(8,128)(2,1)S(1)} %copy-done, s32[1,1024]{1,0:T(1,128)S(1)} %bitcast.20, f32[1,512]{1,0:T(1,128)S(1)} %bitcast.23, f32[1,512]{1,0:T(1,128)S(1)} %bitcast.24), custom_call_target="tpu_custom_call" | custom-call | tf_op jit(solution)/shard_map/pallas_call | solution.py:271
  74.8 0.0 copy-start.3
  74.8 1.3 copy-done.3
  76.1 28.7 %all_to_all.10 = bf16[64,32,128]{2,1,0:T(8,128)(2,1)S(1)} all-to-all(bf16[64,32,128]{2,1,0:T(8,128)(2,1)S(1)} %bitcast.19), channel_id=1, replica_groups=mesh['pts'=64,'head'=4] {'pts'}, dimensions={0} | all-to-all | bytes 1048576 | tf_op jit(solution)/shard_map/all_to_all | solution.py:321
  104.8 2.9 %shard_map.129 = bf16[1024,128]{1,0:T(8,128)(2,1)} custom-call(bf16[2048,128]{1,0:T(8,128)(2,1)S(1)} %bitcast.13), custom_call_target="tpu_custom_call" | custom-call | tf_op jit(solution)/shard_map/pallas_call | solution.py:271
  107.7 0.0 all-gather.9.cloned.1.call-update
  107.7 21.7 %all-gather.9.cloned.1.call-done = bf16[4096,128]{1,0:T(8,128)(2,1)} async-done(((bf16[1024,128]{1,0:T(8,128)(2,1)}), bf16[4096,128]{1,0:T(8,128)(2,1)}) %all-gather.9.cloned.1.call-update) | async-done | bytes 1048592 | tf_op jit(solution)/shard_map/all_gather | solution.py:367
  129.5 0.0 copy-done.9
  129.5 0.0 copy-done.10
  129.5 0.0 copy-done.11
  129.5 1.2 copy-done.7
  130.7 20.0 %shard_map.130 = bf16[2048,128]{1,0:T(8,128)(2,1)} custom-call(bf16[4,1024,128]{2,1,0:T(8,128)(2,1)S(1)} %bitcast.18, bf16[2048,128]{1,0:T(8,128)(2,1)S(1)} %bitcast.14, bf16[512,128]{1,0:T(8,128)(2,1)S(1)} %copy-done.9, bf16[512,128]{1,0:T(8,128)(2,1)S(1)} %copy-done.10, bf16[512,128]{1,0:T(8,128)(2,1)S(1)} %copy-done.11), custom_call_target="tpu_custom_call" | custom-call | tf_op jit(solution)/shard_map/pallas_call | solution.py:271
  150.7 11.7 %all-to-all-start.1 = ((bf16[64,32,128]{2,1,0:T(8,128)(2,1)}), bf16[64,32,128]{2,1,0:T(8,128)(2,1)S(1)}, u32[]{:S(2)}, u32[]{:S(2)}) async-start(bf16[64,32,128]{2,1,0:T(8,128)(2,1)} %bitcast.8), calls=%async_computation.1 | async-start | bytes 1048576 | tf_op jit(solution)/shard_map/all_to_all | solution.py:321
  162.4 0.2 all-gather.11.cloned.1.call-start
  162.6 0.2 copy.16.rank_ref
  162.8 16.9 %all-to-all-done.1 = bf16[64,32,128]{2,1,0:T(8,128)(2,1)S(1)} async-done(((bf16[64,32,128]{2,1,0:T(8,128)(2,1)}), bf16[64,32,128]{2,1,0:T(8,128)(2,1)S(1)}, u32[]{:S(2)}, u32[]{:S(2)}) %all-to-all-start.1) | async-done | bytes 524320 | tf_op jit(solution)/shard_map/all_to_all | solution.py:321
  179.7 3.7 %shard_map.131 = bf16[1024,128]{1,0:T(8,128)(2,1)} custom-call(bf16[2048,128]{1,0:T(8,128)(2,1)S(1)} %bitcast.15, s32[1024,1]{1,0:T(8,128)S(1)} %copy.16.rank_ref), custom_call_target="tpu_custom_call" | custom-call | tf_op jit(solution)/shard_map/pallas_call | solution.py:271
  183.4 0.0 all-gather.11.cloned.1.call-update
  183.4 21.8 %all-gather.11.cloned.1.call-done = bf16[4096,128]{1,0:T(8,128)(2,1)} async-done(((bf16[1024,128]{1,0:T(8,128)(2,1)}), bf16[4096,128]{1,0:T(8,128)(2,1)}) %all-gather.11.cloned.1.call-update) | async-done | bytes 1048592 | tf_op jit(solution)/shard_map/all_gather | solution.py:373
  205.2 0.0 copy-done.2
  205.2 0.0 copy-done.13
  205.2 1.6 copy-done.4
  206.8 1.2 copy-done.5
  208.0 1.0 copy-done.8
  209.0 11.5 %shard_map.132 = bf16[1024,512]{1,0:T(8,128)(2,1)} custom-call(bf16[4,1024,128]{2,1,0:T(8,128)(2,1)S(1)} %bitcast.16, f32[1024,512]{1,0:T(8,128)S(1)} %copy-done.4, bf16[512,512]{1,0:T(8,128)(2,1)S(1)} %copy-done.8, f32[1,512]{1,0:T(1,128)S(1)} %bitcast.22, bf16[512,2048]{1,0:T(8,128)(2,1)S(1)} %copy-done.2, bf16[2048,512]{1,0:T(8,128)(2,1)} %f2_ref.1), custom_call_target="tpu_custom_call" | custom-call | tf_op jit(solution)/shard_map/pallas_call | solution.py:271
  (10 shorter events, 0.0 us)
Async XLA Ops:
  6.5 13.8 %copy-start = (bf16[1024,512]{1,0:T(8,128)(2,1)S(1)}, bf16[1024,512]{1,0:T(8,128)(2,1)}, u32[]{:S(2)}) copy-start(bf16[1024,512]{1,0:T(8,128)(2,1)} %feats_ref.1) | copy-start | bytes 3145732
  6.5 59.8 %all-gather.7.cloned.1.call-start = ((), (), s32[]{:S(2)}) async-start(), calls=%async_computation.2 | async-start | bytes 1310720 | tf_op jit(solution)/shard_map/all_gather | solution.py:353
  7.7 8.2 %collective-permute-start = (bf16[256,512]{1,0:T(8,128)(2,1)S(1)}, bf16[256,512]{1,0:T(8,128)(2,1)S(1)}, u32[]{:S(2)}, u32[]{:S(2)}) collective-permute-start(bf16[256,512]{1,0:T(8,128)(2,1)S(1)} %get-tuple-element.9), channel_id=1, source_target_pairs={{0,4},{4,8},{8,12},{12,16},{16,20},{20,24},{24,28},{28,32},{32,36}... | collective-permute-start | bytes 786440 | tf_op jit(solution)/shard_map/ppermute | solution.py:345
  12.6 7.7 %collective-permute-start.1 = (bf16[256,512]{1,0:T(8,128)(2,1)S(1)}, bf16[256,512]{1,0:T(8,128)(2,1)S(1)}, u32[]{:S(2)}, u32[]{:S(2)}) collective-permute-start(bf16[256,512]{1,0:T(8,128)(2,1)S(1)} %get-tuple-element.10), channel_id=1, source_target_pairs={{4,0},{8,4},{12,8},{16,12},{20,16},{24,20},{28,24},{32,28},{36,32}... | collective-permute-start | bytes 786440 | tf_op jit(solution)/shard_map/ppermute | solution.py:347
  20.4 2.0 copy-start.1
  22.4 43.9 %copy-start.12 = (s32[1024]{0:T(1024)S(1)}, s32[1024]{0:T(1024)}, u32[]{:S(2)}) copy-start(s32[1024]{0:T(1024)} %param.15) | copy-start | bytes 12292
  22.4 43.9 %copy-start.14 = (f32[512]{0:T(512)S(1)}, f32[512]{0:T(512)}, u32[]{:S(2)}) copy-start(f32[512]{0:T(512)} %param.17) | copy-start | bytes 6148
  22.4 43.9 %copy-start.15 = (f32[512]{0:T(512)S(1)}, f32[512]{0:T(512)}, u32[]{:S(2)}) copy-start(f32[512]{0:T(512)} %param.18) | copy-start | bytes 6148
  38.2 91.3 %all-gather.9.cloned.1.call-start = ((), (), s32[]{:S(2)}) async-start(), calls=%async_computation.3 | async-start | bytes 1310720 | tf_op jit(solution)/shard_map/all_gather | solution.py:367
  66.3 1.2 copy-start.6
  67.6 61.9 %copy-start.9 = (bf16[512,128]{1,0:T(8,128)(2,1)S(1)}, bf16[512,128]{1,0:T(8,128)(2,1)}, u32[]{:S(2)}) copy-start(bf16[512,128]{1,0:T(8,128)(2,1)} %wq_ref.1) | copy-start | bytes 393220
  67.6 61.9 %copy-start.10 = (bf16[512,128]{1,0:T(8,128)(2,1)S(1)}, bf16[512,128]{1,0:T(8,128)(2,1)}, u32[]{:S(2)}) copy-start(bf16[512,128]{1,0:T(8,128)(2,1)} %wk_ref.1) | copy-start | bytes 393220
  67.6 61.9 %copy-start.11 = (bf16[512,128]{1,0:T(8,128)(2,1)S(1)}, bf16[512,128]{1,0:T(8,128)(2,1)}, u32[]{:S(2)}) copy-start(bf16[512,128]{1,0:T(8,128)(2,1)} %wv_ref.1) | copy-start | bytes 393220
  74.8 1.4 copy-start.3
  129.5 1.2 copy-start.7
  150.7 54.5 %copy-start.2 = (bf16[512,2048]{1,0:T(8,128)(2,1)S(1)}, bf16[512,2048]{1,0:T(8,128)(2,1)}, u32[]{:S(2)}) copy-start(bf16[512,2048]{1,0:T(8,128)(2,1)} %f1_ref.1) | copy-start | bytes 6291460
  150.7 54.5 %copy-start.13 = (f32[512]{0:T(512)S(1)}, f32[512]{0:T(512)}, u32[]{:S(2)}) copy-start(f32[512]{0:T(512)} %param.23) | copy-start | bytes 6148
  150.7 29.0 %all-to-all-start.1 = ((bf16[64,32,128]{2,1,0:T(8,128)(2,1)}), bf16[64,32,128]{2,1,0:T(8,128)(2,1)S(1)}, u32[]{:S(2)}, u32[]{:S(2)}) async-start(bf16[64,32,128]{2,1,0:T(8,128)(2,1)} %bitcast.8), calls=%async_computation.1 | async-start | bytes 1048576 | tf_op jit(solution)/shard_map/all_to_all | solution.py:321
  162.4 42.8 %all-gather.11.cloned.1.call-start = ((), (), s32[]{:S(2)}) async-start(), calls=%async_computation.4 | async-start | bytes 1310720 | tf_op jit(solution)/shard_map/all_gather | solution.py:373
  205.2 1.6 copy-start.4
  206.8 1.2 copy-start.5
  208.0 1.0 copy-start.8
Sparse Core Ops, SparseCore 0:
  38.3 27.9 all-gather.6
  107.9 21.5 all-gather.8
  183.5 21.5 all-gather.10

commit v2 on v0

v2 whole, which is shorter than its diff:
```python
import jax
import jax.numpy as jnp
import numpy as np
from jax import lax
from jax.experimental import pallas as pl
from jax.experimental.pallas import tpu as pltpu
from jax.sharding import PartitionSpec as P

HD = 16
PTS = 1024
REACH = 256
TAPS = 27
MID = 13
C = 512
MLP = 2048
W = 128
HEADS = 4
DEVS = 64
SLOTS = 32
ROWS = DEVS * SLOTS
NOTE = 16
BLK = 256
CHUNKS = PTS // BLK
GROUP = BLK // SLOTS
BF = jnp.bfloat16
F32 = jnp.float32
I32 = jnp.int32
VMEM = pltpu.MemorySpace.VMEM
MESH = pl.DeviceIdType.MESH


def iota(shape, dim):
    return lax.broadcasted_iota(I32, shape, dim)


def dot(a, b):
    return jnp.dot(a, b, preferred_element_type=F32)


def dot_nt(a, b):
    return lax.dot_general(a, b, (((1,), (1,)), ((), ())), preferred_element_type=F32)


def hot(mask):
    return jnp.where(mask, 1.0, 0.0).astype(BF)


def block(a, size=BLK):
    return pl.ds(pl.multiple_of(a * size, size), size)


def barrier_signal(p, h):
    barrier = pltpu.get_barrier_semaphore()

    @pl.loop(1, DEVS)
    def _(k):
        pl.semaphore_signal(
            barrier, inc=1, device_id=(lax.rem(p + k, DEVS), h), device_id_type=MESH
        )

    for k in (1, HEADS - 1):
        pl.semaphore_signal(
            barrier, inc=1, device_id=(p, lax.rem(h + k, HEADS)), device_id_type=MESH
        )


def barrier_wait():
    pl.semaphore_wait(pltpu.get_barrier_semaphore(), DEVS + 1)


def send_block(p, h, d, size, out_ref, in_ref, send_sem, recv_sem):
    pltpu.make_async_remote_copy(
        src_ref=out_ref.at[block(d, size)],
        dst_ref=in_ref.at[block(p, size)],
        send_sem=send_sem,
        recv_sem=recv_sem,
        device_id=(d, h),
        device_id_type=MESH,
    ).start()


def wait_blocks(size, ref, sem):
    part = ref.at[pl.ds(0, (DEVS - 1) * size)]
    pltpu.make_async_copy(part, part, sem).wait()


class Gather:
    def __init__(self, p, h, ref, send_sem, recv_sem):
        self.p, self.h, self.ref, self.send_sem, self.recv_sem = p, h, ref, send_sem, recv_sem
        self.right, self.left = lax.rem(h + 1, HEADS), lax.rem(h + 3, HEADS)
        self.far = lax.rem(h + 2, HEADS)

    def copy(self, kind, c):
        owner, upper, to = (
            (self.h, True, self.right),
            (self.h, False, self.left),
            (self.h, False, self.right),
            (self.h, True, self.left),
            (self.left, True, self.right),
            (self.right, False, self.left),
        )[kind]
        half = BLK // 2
        start = pl.multiple_of(c * BLK + (0 if upper else half), half)
        rows = self.ref.at[owner, pl.ds(start, half)]
        return pltpu.make_async_remote_copy(
            src_ref=rows,
            dst_ref=rows,
            send_sem=self.send_sem.at[kind, c],
            recv_sem=self.recv_sem.at[kind, c],
            device_id=(self.p, to),
            device_id_type=MESH,
        )

    def start(self, c):
        for kind in range(4):
            self.copy(kind, c).start()

    def relay(self, c):
        self.copy(0, c).wait_recv()
        self.copy(4, c).start()
        self.copy(1, c).wait_recv()
        self.copy(5, c).start()

    def finish(self, c):
        for kind in (2, 3, 4, 5):
            self.copy(kind, c).wait_recv()

    def drain(self):
        @pl.loop(0, CHUNKS)
        def _(c):
            for kind in range(6):
                self.copy(kind, c).wait_send()


def pipelined(gather, produce, consume):
    @pl.loop(0, CHUNKS)
    def _(c):
        produce(c)
        gather.start(c)

        @pl.when(c >= 1)
        def _():
            gather.relay(c - 1)

        @pl.when(c >= 2)
        def _():
            gather.finish(c - 2)
            consume(c - 2)

    gather.relay(CHUNKS - 1)

    @pl.loop(CHUNKS - 2, CHUNKS)
    def _(c):
        gather.finish(c)
        consume(c)


def conv_project(ext_ref, ext_rows, y_rows, w_ref, first, count, y_ref):
    @pl.loop(0, count // 2)
    def _(j):
        pair = jnp.concatenate([w_ref[first + 2 * j], w_ref[first + 2 * j + 1]], 1)
        y = dot(ext_ref[ext_rows, :], pair).astype(BF)
        y_ref[2 * j, y_rows, :] = y[:, :W]
        y_ref[2 * j + 1, y_rows, :] = y[:, W:]

    if count % 2:
        y = dot(ext_ref[ext_rows, :], w_ref[first + count - 1])
        y_ref[count - 1, y_rows, :] = y.astype(BF)


def conv_select(a, base, nbr_ref, yb_ref, yf_ref):
    start = pl.multiple_of(a * BLK, BLK)
    nbr = jnp.transpose(nbr_ref[:, pl.ds(start, BLK)])
    at = jnp.where(nbr < 0, -4096, nbr - (base + start))
    window = iota((BLK, 2 * BLK), 1)
    acc = yb_ref[MID, pl.ds(start + REACH, BLK), :].astype(F32)
    for t in range(TAPS):
        if t < MID:
            sel = hot(window == at[:, t : t + 1] + REACH)
            acc += dot(sel, yb_ref[t, pl.ds(start, 2 * BLK), :])
        elif t > MID:
            sel = hot(window == at[:, t : t + 1])
            acc += dot(sel, yf_ref[t - MID - 1, pl.ds(start, 2 * BLK), :])
    return acc


def norm_slices(parts, gain_ref):
    mean = sum(jnp.sum(p, 1, keepdims=True) for p in parts) * (1.0 / C)
    centre = [p - mean for p in parts]
    spread = sum(jnp.sum(c * c, 1, keepdims=True) for c in centre) * (1.0 / C)
    scale = lax.rsqrt(spread + 1e-05)
    return [c * scale * gain_ref[:, W * k : W * k + W] for k, c in enumerate(centre)]


def mid_block(a, conv_ref, ext_ref, cpe_ref, n1_ref, h1_ref, normed_ref):
    rows = block(a)
    feats = ext_ref[pl.ds(pl.multiple_of(a * BLK + REACH, BLK), BLK), :].astype(F32)
    normed = norm_slices([conv_ref[k, rows, :].astype(F32) for k in range(HEADS)], cpe_ref)
    h1 = [feats[:, W * k : W * k + W] + normed[k] for k in range(HEADS)]
    for k, part in enumerate(norm_slices(h1, n1_ref)):
        h1_ref[rows, W * k : W * k + W] = h1[k]
        normed_ref[k, rows, :] = part.astype(BF)


def column_of(row):
    same = iota((W, W), 0) == iota((W, W), 1)
    parts = [
        jnp.sum(jnp.where(same, row[:, k : k + W], 0), 1, keepdims=True)
        for k in range(0, row.shape[1], W)
    ]
    return jnp.concatenate(parts, 0)


def bucket_of(rank_row):
    target = rank_row // PTS
    member = iota((DEVS, PTS), 0) == target
    ones = jnp.where(member, 1.0, 0.0)
    upper = hot(iota((PTS, PTS), 0) < iota((PTS, PTS), 1))
    counts = dot(ones.astype(BF), upper)
    slot = jnp.sum(counts * ones, 0, keepdims=True).astype(I32)
    code = rank_row % PTS + 1
    by_slot = hot(iota((W, PTS), 0) == slot)
    high = dot_nt((ones * (code // 32).astype(F32)).astype(BF), by_slot)
    low = dot_nt((ones * (code % 32).astype(F32)).astype(BF), by_slot)
    return target * SLOTS + slot, jnp.concatenate([high, low], 0).astype(BF)


def note_rows(positions):
    r = iota((DEVS * NOTE, W), 0)
    c = iota((DEVS * NOTE, W), 1)
    d = r // NOTE
    place = hot(((r % NOTE == 0) & (c == d)) | ((r % NOTE == 1) & (c == d + DEVS)))
    return dot(place, positions).astype(BF)


def spots_of(notes):
    r = iota((DEVS, DEVS * NOTE), 1)
    q = iota((DEVS, DEVS * NOTE), 0)
    high = dot(hot(r == q * NOTE), notes).astype(BF)
    low = dot(hot(r == q * NOTE + 1), notes).astype(BF)
    pick = hot(iota((W, ROWS), 0) == iota((W, ROWS), 1) % SLOTS)
    full = dot(high, pick) * 32.0 + dot(low, pick) - 1.0
    mine = iota((DEVS, ROWS), 0) == iota((DEVS, ROWS), 1) // SLOTS
    return jnp.sum(jnp.where(mine, full, 0.0), 0, keepdims=True).astype(I32)


def project_qkv(rows, x_ref, wq_ref, wk_ref, wv_ref, qq_ref, k_ref, v_ref):
    def project(w_ref):
        parts = [dot(x_ref[k, rows, :], w_ref[W * k : W * k + W, :]) for k in range(HEADS)]
        return sum(parts).astype(BF)

    scaled = project(wq_ref).astype(F32) * np.float32(np.log2(np.e) / 4.0)
    high = scaled.astype(BF)
    qq_ref[rows, :W] = high
    qq_ref[rows, W:] = (scaled - high.astype(F32)).astype(BF)
    k_ref[rows, :] = project(wk_ref)
    v_ref[rows, :] = project(wv_ref)


def attend(qq_ref, k_ref, v_ref, acc_ref, att_ref):
    acc_ref[...] = jnp.zeros_like(acc_ref)
    lane = iota((PTS, W), 1) // HD

    @pl.loop(0, W // HD)
    def _(head):
        own = lane == head
        zero = jnp.zeros((PTS, W), BF)
        keys = jnp.where(own, k_ref[...], zero)
        keys = jnp.concatenate([keys, keys], 1)
        values = jnp.concatenate([jnp.where(own, v_ref[...], zero), hot(own)], 1)
        for b in range(CHUNKS):
            rows = slice(b * BLK, b * BLK + BLK)
            scores = dot_nt(qq_ref[rows, :], keys)
            top = jnp.max(scores, 1, keepdims=True)
            probs = jnp.exp2(scores - top).astype(BF)
            acc_ref[rows, :] += dot(probs, values)

    att_ref[...] = (acc_ref[:, :W] / acc_ref[:, W:]).astype(BF)


def mlp_block(a, att_ref, h1_ref, wp_ref, n2_ref, f1_ref, f2_ref, out_ref):
    rows = block(a)
    merged = sum(dot(att_ref[k, rows, :], wp_ref[W * k : W * k + W, :]) for k in range(HEADS))
    h2 = h1_ref[rows, :] + merged.astype(BF).astype(F32)
    parts = norm_slices([h2[:, W * k : W * k + W] for k in range(HEADS)], n2_ref)
    normed = jnp.concatenate([part.astype(BF) for part in parts], 1)
    total = h2
    for j in range(MLP // C):
        cols = slice(C * j, C * j + C)
        x = dot(normed, f1_ref[:, cols])
        hidden = (0.5 * x * (1.0 + lax.erf(x * np.float32(np.sqrt(0.5))))).astype(BF)
        total += dot(hidden, f2_ref[cols, :])
    out_ref[rows, :] = total.astype(BF)


def whole_kernel(
    feats_hbm,
    nbr_ref,
    rank_ref,
    cw_hbm,
    cpe_ref,
    n1_ref,
    wq_hbm,
    wk_hbm,
    wv_hbm,
    wp_hbm,
    n2_ref,
    f1_hbm,
    f2_hbm,
    out_hbm,
    ext,
    cw,
    wq,
    wk,
    wv,
    wp,
    f1,
    f2,
    yb,
    yf,
    conv_all,
    placed_all,
    merged_all,
    h1,
    normed,
    note_out,
    note_in,
    there_out,
    there_in,
    back_out,
    back_in,
    to_place,
    from_place,
    from_bucket,
    qq,
    keys,
    values,
    acc,
    att,
    result,
    load_sem,
    halo_send,
    halo_recv,
    block_send,
    block_recv,
    gather_send,
    gather_recv,
    store_sem,
):
    p = lax.axis_index("pts")
    h = lax.axis_index("head")
    loads = [
        pltpu.make_async_copy(source, target, load_sem.at[i])
        for i, (source, target) in enumerate(
            (
                (feats_hbm, ext.at[pl.ds(REACH, PTS)]),
                (cw_hbm, cw),
                (wq_hbm, wq),
                (wk_hbm, wk),
                (wv_hbm, wv),
                (wp_hbm, wp),
                (f1_hbm, f1),
                (f2_hbm, f2),
            )
        )
    ]
    for load in loads:
        load.start()
    barrier_signal(p, h)
    bucket, positions = bucket_of(rank_ref[...])
    note_out[...] = note_rows(positions)
    barrier_wait()

    halos = [
        pltpu.make_async_remote_copy(
            src_ref=feats_hbm.at[pl.ds(first, REACH)],
            dst_ref=ext.at[pl.ds(to, REACH)],
            send_sem=halo_send.at[i],
            recv_sem=halo_recv.at[i],
            device_id=(lax.rem(p + step, DEVS), h),
            device_id_type=MESH,
        )
        for i, (first, to, step) in enumerate(
            ((PTS - REACH, 0, 1), (0, PTS + REACH, DEVS - 1))
        )
    ]
    for halo in halos:
        halo.start()

    @pl.loop(1, DEVS)
    def _(k):
        d = lax.rem(p + k, DEVS)
        send_block(p, h, d, NOTE, note_out, note_in, block_send.at[0], block_recv.at[0])

    note_in[block(p, NOTE), :] = note_out[block(p, NOTE), :]

    loads[0].wait()
    loads[1].wait()
    inner = pl.ds(REACH, PTS)
    conv_project(ext, inner, inner, cw, 0, MID + 1, yb)
    conv_project(ext, inner, pl.ds(0, PTS), cw, MID + 1, MID, yf)
    for halo in halos:
        halo.wait_recv()
    conv_project(ext, pl.ds(0, REACH), pl.ds(0, REACH), cw, 0, MID, yb)
    after = pl.ds(PTS + REACH, REACH)
    conv_project(ext, after, pl.ds(PTS, REACH), cw, MID + 1, MID, yf)

    def convolve(c):
        conv_all[h, block(c), :] = conv_select(c, p * PTS, nbr_ref, yb, yf).astype(BF)

    def norm(c):
        mid_block(c, conv_all, ext, cpe_ref, n1_ref, h1, normed)

    gathers = [
        Gather(p, h, ref, gather_send.at[i], gather_recv.at[i])
        for i, ref in enumerate((conv_all, placed_all, merged_all))
    ]
    pipelined(gathers[0], convolve, norm)

    def scatter(make, out_ref, in_ref, send_sem, recv_sem):
        @pl.loop(0, ROWS // BLK)
        def _(j):
            b = lax.rem(p // GROUP + j, ROWS // BLK)
            out_ref[block(b), :] = make(b).astype(BF)

            @pl.loop(0, GROUP)
            def _(i):
                d = b * GROUP + lax.rem(p + i, GROUP)

                @pl.when(d != p)
                def _():
                    send_block(p, h, d, SLOTS, out_ref, in_ref, send_sem, recv_sem)

        in_ref[block(p, SLOTS), :] = out_ref[block(p, SLOTS), :]

    def pack(b):
        return dot(hot(iota((BLK, PTS), 0) + b * BLK == bucket), normed[h])

    scatter(pack, there_out, there_in, block_send.at[1], block_recv.at[1])
    wait_blocks(NOTE, note_in, block_recv.at[0])
    spots = spots_of(note_in[...])

    @pl.loop(0, CHUNKS)
    def _(c):
        to_place[block(c), :] = hot(iota((BLK, ROWS), 0) + c * BLK == spots)

    spots_column = column_of(spots)
    for k in range(0, ROWS, BLK):
        from_place[k : k + BLK, :] = hot(iota((BLK, PTS), 1) == spots_column[k : k + BLK, :])
    wait_blocks(SLOTS, there_in, block_recv.at[1])
    for load in loads[2:5]:
        load.wait()

    def place(c):
        placed_all[h, block(c), :] = dot(to_place[block(c), :], there_in[...]).astype(BF)

    def project(c):
        project_qkv(block(c), placed_all, wq, wk, wv, qq, keys, values)

    pipelined(gathers[1], place, project)
    attend(qq, keys, values, acc, att)

    def unplace(b):
        return dot(from_place[block(b), :], att[...])

    scatter(unplace, back_out, back_in, block_send.at[2], block_recv.at[2])
    bucket_column = column_of(bucket)
    for k in range(0, PTS, BLK):
        from_bucket[k : k + BLK, :] = hot(iota((BLK, ROWS), 1) == bucket_column[k : k + BLK, :])
    wait_blocks(SLOTS, back_in, block_recv.at[2])
    for load in loads[5:]:
        load.wait()

    def unpack(c):
        merged_all[h, block(c), :] = dot(from_bucket[block(c), :], back_in[...]).astype(BF)

    def store(c):
        return pltpu.make_async_copy(
            result.at[block(c)], out_hbm.at[block(c)], store_sem.at[c]
        )

    def perceive(c):
        mlp_block(c, merged_all, h1, wp, n2_ref, f1, f2, result)
        store(c).start()

    pipelined(gathers[2], unpack, perceive)

    for halo in halos:
        halo.wait_send()
    for i, (size, ref) in enumerate(((NOTE, note_out), (SLOTS, there_out), (SLOTS, back_out))):
        wait_blocks(size, ref, block_send.at[i])
    for gather in gathers:
        gather.drain()

    @pl.loop(0, CHUNKS)
    def _(c):
        store(c).wait()


def per_device(
    feats,
    neighbours,
    rank,
    conv_weight,
    cpe_gain,
    norm1_gain,
    w_query,
    w_key,
    w_value,
    w_proj,
    norm2_gain,
    w_fc1,
    w_fc2,
):
    here, there = pl.BlockSpec(memory_space=VMEM), pl.BlockSpec(memory_space=pl.ANY)
    dma = pltpu.SemaphoreType.DMA
    return pl.pallas_call(
        whole_kernel,
        out_shape=jax.ShapeDtypeStruct((PTS, C), BF),
        in_specs=[there, here, here, there, here, here] + [there] * 4 + [here, there, there],
        out_specs=there,
        scratch_shapes=[
            pltpu.VMEM((PTS + 2 * REACH, C), BF),
            pltpu.VMEM((TAPS, C, W), BF),
            pltpu.VMEM((C, W), BF),
            pltpu.VMEM((C, W), BF),
            pltpu.VMEM((C, W), BF),
            pltpu.VMEM((C, C), BF),
            pltpu.VMEM((C, MLP), BF),
            pltpu.VMEM((MLP, C), BF),
            pltpu.VMEM((MID + 1, PTS + REACH, W), BF),
            pltpu.VMEM((MID, PTS + REACH, W), BF),
            pltpu.VMEM((HEADS, PTS, W), BF),
            pltpu.VMEM((HEADS, PTS, W), BF),
            pltpu.VMEM((HEADS, PTS, W), BF),
            pltpu.VMEM((PTS, C), F32),
            pltpu.VMEM((HEADS, PTS, W), BF),
            pltpu.VMEM((DEVS * NOTE, W), BF),
            pltpu.VMEM((DEVS * NOTE, W), BF),
            pltpu.VMEM((ROWS, W), BF),
            pltpu.VMEM((ROWS, W), BF),
            pltpu.VMEM((ROWS, W), BF),
            pltpu.VMEM((ROWS, W), BF),
            pltpu.VMEM((PTS, ROWS), BF),
            pltpu.VMEM((ROWS, PTS), BF),
            pltpu.VMEM((PTS, ROWS), BF),
            pltpu.VMEM((PTS, 2 * W), BF),
            pltpu.VMEM((PTS, W), BF),
            pltpu.VMEM((PTS, W), BF),
            pltpu.VMEM((PTS, 2 * W), F32),
            pltpu.VMEM((PTS, W), BF),
            pltpu.VMEM((PTS, C), BF),
            dma((8,)),
            dma((2,)),
            dma((2,)),
            dma((3,)),
            dma((3,)),
            dma((3, 6, CHUNKS)),
            dma((3, 6, CHUNKS)),
            dma((CHUNKS,)),
        ],
        compiler_params=pltpu.CompilerParams(
            collective_id=0, has_side_effects=True, vmem_limit_bytes=58 * 2**20
        ),
    )(
        feats,
        neighbours.T,
        rank.reshape(1, PTS),
        conv_weight,
        cpe_gain.reshape(1, C),
        norm1_gain.reshape(1, C),
        w_query,
        w_key,
        w_value,
        w_proj,
        norm2_gain.reshape(1, C),
        w_fc1,
        w_fc2,
    )


def solution(mesh):
    placed = (
        P("pts", None),
        P("pts", None),
        P("pts"),
        P(None, None, "head"),
        P(),
        P(),
        P(None, "head"),
        P(None, "head"),
        P(None, "head"),
        P(),
        P(),
        P(),
        P(),
    )
    return jax.shard_map(
        per_device, mesh=mesh, in_specs=placed, out_specs=P("pts", None), check_vma=False
    )
```

time: 532 us -> 120 us (0.23)
  local copies, waits for them, and re-layouts: 203 us -> 2.26 us
  Pallas kernels: 0 us -> 116 us
  matrix products: 107 us -> 0 us
  waiting for transfers between devices: 84.4 us -> 0 us
  blocking collectives: 62.7 us -> 0 us
  starting transfers between devices: 31.3 us -> 0 us
  other arithmetic: 23.5 us -> 0 us
  between operations: 14 us -> 0.01 us
    gather x5 -> x0, local copies, waits for them, and re-layouts: 173 us -> none  [the longest x2 159 us: per_device(): stacked = padded[local_rows].reshape(points, taps * width)]
    pallas_call x0 -> x1, Pallas kernels: none -> 116 us  [per_device(): pl.pallas_call(whole_kernel, out_shape=jax.ShapeDtypeStruct((PTS, C), BF)...]
    dot_general x8 -> x0, matrix products: 92 us -> none  [the longest x1 49.1 us: per_device(): jnp.dot(stacked, conv_weight.reshape(taps * width, head_width), preferred...]
    all_to_all x1 -> x0, blocking collectives: 62.7 us -> none  [per_device(): lax.all_to_all(rows_back.reshape(devices, capacity, merged_owner.shape[1]...]
    all_to_all x2 -> x0, waiting for transfers between devices: 49.8 us -> none  [the longest x1 49.8 us: per_device(): lax.all_to_all(outgoing, 'pts', split_axis=0, concat_axis=0, tiled=True)]
    all_gather x2 -> x0, waiting for transfers between devices: 34.6 us -> none  [the longest x1 21.7 us: per_device(): lax.all_gather(attended, 'head', axis=1, tiled=True)]
    all_to_all x2 -> x0, starting transfers between devices: 24.1 us -> none  [the longest x1 12.6 us: per_device(): lax.all_to_all(spots_out, 'pts', split_axis=0, concat_axis=0, tiled=True)]
    scatter x2 -> x0, local copies, waits for them, and re-layouts: 15.4 us -> none  [the longest x1 11.1 us: per_device(): jnp.zeros((points, flat.shape[1]), jnp.bfloat16).at[chosen]]
  transfers between devices with their start and end apart: 6 -> 0, of which waited for: 3 -> 0; matrix products, arithmetic and copies ran while one was open for 6% -> 0% of each run, Pallas kernels for 0% -> 0%
where the time goes in v2:
time: 120 us; the launch traced here: 118 us
  Pallas kernels  116 us (97%)
  local copies, waits for them, and re-layouts  2.26 us (2%)
    pallas_call x1, Pallas kernels, per_device(): pl.pallas_call(whole_kernel, out_shape=jax.ShapeDtypeStruct((PTS, C), BF)...  116 us

profile of v2, /device:TPU:1, one launch (start us, length us, event | category | flops | bytes accessed | tf_op | source)
XLA Modules:
  0.0 118.0 jit_solution(4307645191598068359)
XLA Ops:
  0.0 115.7 %shard_map.127 = bf16[1024,512]{1,0:T(8,128)(2,1)} custom-call(bf16[1024,512]{1,0:T(8,128)(2,1)} %feats_hbm.1, s32[27,1024]{1,0:T(8,128)} %bitcast.5, s32[1,1024]{1,0:T(1,128)} %bitcast.6, bf16[27,512,128]{2,1,0:T(8,128)(2,1)} %cw_hbm.1, f32[1,512]{1,0:T(1,128)} %bitcast.7, f32[1,512]{1,0:T(1,128)} %bitcast.8, bf16[512,128]{1,0:T(8,128)(2,1)} %wq_hbm.1, ...), custom_call_target="tpu_custom_call" | custom-call | tf_op jit(solution)/shard_map/pallas_call | solution.py:517
  115.7 2.3 %copy.15 = bf16[1024,512]{1,0:T(8,128)(2,1)} copy(bf16[1024,512]{1,0:T(8,128)(2,1)} %shard_map.127) | data formatting | bytes 2097152

commit v3 on v2

--- a/solution.py
+++ b/solution.py
@@ -17,11 +17,14 @@
 HEADS = 4
 DEVS = 64
 SLOTS = 32
+HALF = SLOTS // 2
+SIDE = DEVS * HALF
 ROWS = DEVS * SLOTS
+WAVE = 64
 NOTE = 16
 BLK = 256
 CHUNKS = PTS // BLK
-GROUP = BLK // SLOTS
+GROUP = BLK // HALF
 BF = jnp.bfloat16
 F32 = jnp.float32
 I32 = jnp.int32
@@ -43,6 +46,14 @@
 
 def hot(mask):
     return jnp.where(mask, 1.0, 0.0).astype(BF)
+
+
+def turned(x):
+    return pltpu.roll(x.astype(F32), WAVE, 1).astype(x.dtype)
+
+
+def beside(low, high):
+    return jnp.where(iota(low.shape, 1) < WAVE, low, high)
 
 
 def block(a, size=BLK):
@@ -88,7 +99,7 @@
     def __init__(self, p, h, ref, send_sem, recv_sem):
         self.p, self.h, self.ref, self.send_sem, self.recv_sem = p, h, ref, send_sem, recv_sem
         self.right, self.left = lax.rem(h + 1, HEADS), lax.rem(h + 3, HEADS)
-        self.far = lax.rem(h + 2, HEADS)
+        self.half = ref.shape[1] // CHUNKS // 2
 
     def copy(self, kind, c):
         owner, upper, to = (
@@ -99,9 +110,8 @@
             (self.left, True, self.right),
             (self.right, False, self.left),
         )[kind]
-        half = BLK // 2
-        start = pl.multiple_of(c * BLK + (0 if upper else half), half)
-        rows = self.ref.at[owner, pl.ds(start, half)]
+        start = pl.multiple_of((2 * c + (0 if upper else 1)) * self.half, self.half)
+        rows = self.ref.at[owner, pl.ds(start, self.half)]
         return pltpu.make_async_remote_copy(
             src_ref=rows,
             dst_ref=rows,
@@ -132,40 +142,15 @@
                 self.copy(kind, c).wait_send()
 
 
-def pipelined(gather, produce, consume):
-    @pl.loop(0, CHUNKS)
-    def _(c):
-        produce(c)
-        gather.start(c)
-
-        @pl.when(c >= 1)
-        def _():
-            gather.relay(c - 1)
-
-        @pl.when(c >= 2)
-        def _():
-            gather.finish(c - 2)
-            consume(c - 2)
-
-    gather.relay(CHUNKS - 1)
-
-    @pl.loop(CHUNKS - 2, CHUNKS)
-    def _(c):
-        gather.finish(c)
-        consume(c)
-
-
 def conv_project(ext_ref, ext_rows, y_rows, w_ref, first, count, y_ref):
-    @pl.loop(0, count // 2)
-    def _(j):
-        pair = jnp.concatenate([w_ref[first + 2 * j], w_ref[first + 2 * j + 1]], 1)
-        y = dot(ext_ref[ext_rows, :], pair).astype(BF)
-        y_ref[2 * j, y_rows, :] = y[:, :W]
-        y_ref[2 * j + 1, y_rows, :] = y[:, W:]
-
-    if count % 2:
-        y = dot(ext_ref[ext_rows, :], w_ref[first + count - 1])
-        y_ref[count - 1, y_rows, :] = y.astype(BF)
+    for j in range(0, count, 2):
+        if j + 1 < count:
+            pair = jnp.concatenate([w_ref[first + j], w_ref[first + j + 1]], 1)
+            y = dot(ext_ref[ext_rows, :], pair).astype(BF)
+            y_ref[j, y_rows, :] = y[:, :W]
+            y_ref[j + 1, y_rows, :] = y[:, W:]
+        else:
+            y_ref[j, y_rows, :] = dot(ext_ref[ext_rows, :], w_ref[first + j]).astype(BF)
 
 
 def conv_select(a, base, nbr_ref, yb_ref, yf_ref):
@@ -222,7 +207,8 @@
     by_slot = hot(iota((W, PTS), 0) == slot)
     high = dot_nt((ones * (code // 32).astype(F32)).astype(BF), by_slot)
     low = dot_nt((ones * (code % 32).astype(F32)).astype(BF), by_slot)
-    return target * SLOTS + slot, jnp.concatenate([high, low], 0).astype(BF)
+    row = slot // HALF * SIDE + target * HALF + slot % HALF
+    return row, jnp.concatenate([high, low], 0).astype(BF)
 
 
 def note_rows(positions):
@@ -238,59 +224,97 @@
     q = iota((DEVS, DEVS * NOTE), 0)
     high = dot(hot(r == q * NOTE), notes).astype(BF)
     low = dot(hot(r == q * NOTE + 1), notes).astype(BF)
-    pick = hot(iota((W, ROWS), 0) == iota((W, ROWS), 1) % SLOTS)
+    row = iota((W, ROWS), 1)
+    pick = hot(iota((W, ROWS), 0) == row // SIDE * HALF + row % HALF)
     full = dot(high, pick) * 32.0 + dot(low, pick) - 1.0
-    mine = iota((DEVS, ROWS), 0) == iota((DEVS, ROWS), 1) // SLOTS
+    mine = iota((DEVS, ROWS), 0) == iota((DEVS, ROWS), 1) % SIDE // HALF
     return jnp.sum(jnp.where(mine, full, 0.0), 0, keepdims=True).astype(I32)
 
 
-def project_qkv(rows, x_ref, wq_ref, wk_ref, wv_ref, qq_ref, k_ref, v_ref):
-    def project(w_ref):
-        parts = [dot(x_ref[k, rows, :], w_ref[W * k : W * k + W, :]) for k in range(HEADS)]
-        return sum(parts).astype(BF)
-
-    scaled = project(wq_ref).astype(F32) * np.float32(np.log2(np.e) / 4.0)
+def joined(c, ref):
+    rows = block(c, BLK // 2)
+    parts = []
+    for k in range(HEADS):
+        first, last = ref[0, k, rows, :], ref[1, k, rows, :]
+        parts.append(
+            jnp.concatenate([beside(first, turned(last)), beside(turned(first), last)], 0)
+        )
+    return jnp.concatenate(parts, 1)
+
+
+def project_qkv(c, x_ref, w_ref, qq_ref, k_ref, v_ref):
+    rows = block(c)
+    qkv = dot(joined(c, x_ref), w_ref[...]).astype(BF)
+    scaled = qkv[:, :W].astype(F32) * np.float32(np.log2(np.e) / 4.0)
     high = scaled.astype(BF)
     qq_ref[rows, :W] = high
     qq_ref[rows, W:] = (scaled - high.astype(F32)).astype(BF)
-    k_ref[rows, :] = project(wk_ref)
-    v_ref[rows, :] = project(wv_ref)
-
-
-def attend(qq_ref, k_ref, v_ref, acc_ref, att_ref):
+    k_ref[rows, :] = qkv[:, W : 2 * W]
+    v_ref[rows, :] = qkv[:, 2 * W :]
+
+
+def attend(wave, qq_ref, k_ref, v_ref, acc_ref, att_ref):
     acc_ref[...] = jnp.zeros_like(acc_ref)
     lane = iota((PTS, W), 1) // HD
-
-    @pl.loop(0, W // HD)
-    def _(head):
+    heads = WAVE // HD
+
+    def operands(head):
         own = lane == head
         zero = jnp.zeros((PTS, W), BF)
         keys = jnp.where(own, k_ref[...], zero)
-        keys = jnp.concatenate([keys, keys], 1)
-        values = jnp.concatenate([jnp.where(own, v_ref[...], zero), hot(own)], 1)
-        for b in range(CHUNKS):
-            rows = slice(b * BLK, b * BLK + BLK)
-            scores = dot_nt(qq_ref[rows, :], keys)
+        values = jnp.where(own, v_ref[...], zero)
+        return jnp.concatenate([keys, keys], 1), jnp.concatenate([values, hot(own)], 1)
+
+    @pl.loop(wave * heads, wave * heads + heads, step=2)
+    def _(first):
+        pairs = [operands(first), operands(first + 1)]
+        steps = [(pair, slice(b * BLK, b * BLK + BLK)) for pair in pairs for b in range(CHUNKS)]
+        coming = dot_nt(qq_ref[steps[0][1], :], steps[0][0][0])
+        for i, ((_, values), rows) in enumerate(steps):
+            scores = coming
+            if i + 1 < len(steps):
+                (keys, _), later = steps[i + 1]
+                coming = dot_nt(qq_ref[later, :], keys)
             top = jnp.max(scores, 1, keepdims=True)
             probs = jnp.exp2(scores - top).astype(BF)
             acc_ref[rows, :] += dot(probs, values)
 
-    att_ref[...] = (acc_ref[:, :W] / acc_ref[:, W:]).astype(BF)
-
-
-def mlp_block(a, att_ref, h1_ref, wp_ref, n2_ref, f1_ref, f2_ref, out_ref):
-    rows = block(a)
-    merged = sum(dot(att_ref[k, rows, :], wp_ref[W * k : W * k + W, :]) for k in range(HEADS))
-    h2 = h1_ref[rows, :] + merged.astype(BF).astype(F32)
+    done = lane // heads == wave
+    straight = jnp.where(done, acc_ref[:, :W] / jnp.where(done, acc_ref[:, W:], 1.0), 0.0)
+    other = pltpu.roll(straight, WAVE, 1)
+    first, last = (other, straight) if wave else (straight, other)
+    att_ref[:, :W] = first.astype(BF)
+    att_ref[:, W:] = last.astype(BF)
+
+
+def gelu(x):
+    return 0.5 * x * (1.0 + lax.erf(x * np.float32(np.sqrt(0.5))))
+
+
+def mlp_rows(a, att_ref, h1_ref, wp_ref, n2_ref):
+    merged = dot(joined(a, att_ref), wp_ref[...])
+    h2 = h1_ref[block(a), :] + merged.astype(BF).astype(F32)
     parts = norm_slices([h2[:, W * k : W * k + W] for k in range(HEADS)], n2_ref)
-    normed = jnp.concatenate([part.astype(BF) for part in parts], 1)
-    total = h2
-    for j in range(MLP // C):
-        cols = slice(C * j, C * j + C)
-        x = dot(normed, f1_ref[:, cols])
-        hidden = (0.5 * x * (1.0 + lax.erf(x * np.float32(np.sqrt(0.5))))).astype(BF)
-        total += dot(hidden, f2_ref[cols, :])
-    out_ref[rows, :] = total.astype(BF)
+    return h2, jnp.concatenate([part.astype(BF) for part in parts], 1)
+
+
+def mlp_blocks(chunks, att_ref, h1_ref, wp_ref, n2_ref, f1_ref, f2_ref, out_ref):
+    width = C // 2
+    steps = [(i, slice(j, j + width)) for i in range(len(chunks)) for j in range(0, MLP, width)]
+    ready = [mlp_rows(chunks[0], att_ref, h1_ref, wp_ref, n2_ref)]
+    total = [ready[0][0]]
+    coming = dot(ready[0][1], f1_ref[:, steps[0][1]])
+    for n, (i, cols) in enumerate(steps):
+        x = coming
+        if n + 3 < len(steps) and steps[n + 3][0] == len(ready):
+            ready.append(mlp_rows(chunks[len(ready)], att_ref, h1_ref, wp_ref, n2_ref))
+            total.append(ready[-1][0])
+        if n + 1 < len(steps):
+            later, ahead = steps[n + 1]
+            coming = dot(ready[later][1], f1_ref[:, ahead])
+        total[i] += dot(gelu(x).astype(BF), f2_ref[cols, :])
+        if cols.stop == MLP:
+            out_ref[block(chunks[i]), :] = total[i].astype(BF)
 
 
 def whole_kernel(
@@ -310,9 +334,7 @@
     out_hbm,
     ext,
     cw,
-    wq,
-    wk,
-    wv,
+    wqkv,
     wp,
     f1,
     f2,
@@ -355,9 +377,9 @@
             (
                 (feats_hbm, ext.at[pl.ds(REACH, PTS)]),
                 (cw_hbm, cw),
-                (wq_hbm, wq),
-                (wk_hbm, wk),
-                (wv_hbm, wv),
+                (wq_hbm, wqkv.at[:, pl.ds(0, W)]),
+                (wk_hbm, wqkv.at[:, pl.ds(W, W)]),
+                (wv_hbm, wqkv.at[:, pl.ds(2 * W, W)]),
                 (wp_hbm, wp),
                 (f1_hbm, f1),
                 (f2_hbm, f2),
@@ -369,6 +391,10 @@
     barrier_signal(p, h)
     bucket, positions = bucket_of(rank_ref[...])
     note_out[...] = note_rows(positions)
+    loads[0].wait()
+    loads[1].wait()
+    inner = pl.ds(REACH, PTS)
+    conv_project(ext, inner, inner, cw, 0, MID + 1, yb)
     barrier_wait()
 
     halos = [
@@ -386,6 +412,30 @@
     ]
     for halo in halos:
         halo.start()
+    conv_project(ext, inner, pl.ds(0, PTS), cw, MID + 1, MID, yf)
+
+    gathers = [
+        Gather(p, h, ref, gather_send.at[i], gather_recv.at[i])
+        for i, ref in enumerate(
+            [conv_all] + [ref.at[w] for ref in (placed_all, merged_all) for w in range(2)]
+        )
+    ]
+    gather = gathers[0]
+
+    def convolve(c):
+        conv_all[h, block(c), :] = conv_select(c, p * PTS, nbr_ref, yb, yf).astype(BF)
+        gather.start(c)
+
+    def norm(c):
+        gather.finish(c)
+        mid_block(c, conv_all, ext, cpe_ref, n1_ref, h1, normed)
+
+    @pl.loop(1, 3)
+    def _(c):
+        convolve(c)
+
+    for halo in halos:
+        halo.wait_recv()
 
     @pl.loop(1, DEVS)
     def _(k):
@@ -394,49 +444,67 @@
 
     note_in[block(p, NOTE), :] = note_out[block(p, NOTE), :]
 
-    loads[0].wait()
-    loads[1].wait()
-    inner = pl.ds(REACH, PTS)
-    conv_project(ext, inner, inner, cw, 0, MID + 1, yb)
-    conv_project(ext, inner, pl.ds(0, PTS), cw, MID + 1, MID, yf)
-    for halo in halos:
-        halo.wait_recv()
     conv_project(ext, pl.ds(0, REACH), pl.ds(0, REACH), cw, 0, MID, yb)
     after = pl.ds(PTS + REACH, REACH)
     conv_project(ext, after, pl.ds(PTS, REACH), cw, MID + 1, MID, yf)
-
-    def convolve(c):
-        conv_all[h, block(c), :] = conv_select(c, p * PTS, nbr_ref, yb, yf).astype(BF)
-
-    def norm(c):
-        mid_block(c, conv_all, ext, cpe_ref, n1_ref, h1, normed)
-
-    gathers = [
-        Gather(p, h, ref, gather_send.at[i], gather_recv.at[i])
-        for i, ref in enumerate((conv_all, placed_all, merged_all))
-    ]
-    pipelined(gathers[0], convolve, norm)
-
-    def scatter(make, out_ref, in_ref, send_sem, recv_sem):
-        @pl.loop(0, ROWS // BLK)
-        def _(j):
-            b = lax.rem(p // GROUP + j, ROWS // BLK)
-            out_ref[block(b), :] = make(b).astype(BF)
-
-            @pl.loop(0, GROUP)
-            def _(i):
-                d = b * GROUP + lax.rem(p + i, GROUP)
-
-                @pl.when(d != p)
-                def _():
-                    send_block(p, h, d, SLOTS, out_ref, in_ref, send_sem, recv_sem)
-
-        in_ref[block(p, SLOTS), :] = out_ref[block(p, SLOTS), :]
-
-    def pack(b):
-        return dot(hot(iota((BLK, PTS), 0) + b * BLK == bucket), normed[h])
-
-    scatter(pack, there_out, there_in, block_send.at[1], block_recv.at[1])
+    gather.relay(1)
+    gather.relay(2)
+
+    @pl.loop(0, 2)
+    def _(j):
+        convolve(3 * j)
+        norm(1 + j)
+
+    gather.relay(0)
+    gather.relay(3)
+    norm(0)
+    norm(3)
+
+    x, z, core = p // GROUP, lax.rem(p, GROUP) // 2, lax.rem(p, 2)
+
+    def send_wave(w, b, out_ref, in_ref, i):
+        def send(d):
+            send_block(
+                p, h, d, HALF, out_ref.at[w], in_ref.at[w],
+                block_send.at[i + w], block_recv.at[i + w],
+            )
+
+        for ahead in (4, 3, 5, 2, 6, 1, 7):
+            chip = b * GROUP + 2 * lax.rem(z + ahead, GROUP // 2)
+            send(chip)
+            send(chip + 1)
+        chip = b * GROUP + 2 * z
+        send(chip + 1 - core)
+
+        @pl.when(b != x)
+        def _():
+            send(chip + core)
+
+    def turn_of(j):
+        return lax.rem(x + 2 + 3 * j, CHUNKS)
+
+    def keep_own(w, out_ref, in_ref):
+        in_ref[w, block(p, HALF), :] = out_ref[w, block(p, HALF), :]
+
+    own = normed[h]
+    own = jnp.concatenate([own, turned(own)], 1)
+
+    @pl.loop(0, CHUNKS)
+    def _(j):
+        b = turn_of(j)
+        row = iota((BLK, PTS), 0) + b * BLK
+        low = dot(hot(row == bucket), own)
+        high = dot(hot(row + SIDE == bucket), own)
+        there_out[0, block(b), :] = beside(low[:, :W], high[:, W:]).astype(BF)
+        there_out[1, block(b), :] = beside(low[:, W:], high[:, :W]).astype(BF)
+        send_wave(0, b, there_out, there_in, 1)
+
+    @pl.loop(0, CHUNKS)
+    def _(j):
+        send_wave(1, turn_of(j), there_out, there_in, 1)
+
+    for w in range(2):
+        keep_own(w, there_out, there_in)
     wait_blocks(NOTE, note_in, block_recv.at[0])
     spots = spots_of(note_in[...])
 
@@ -444,56 +512,83 @@
     def _(c):
         to_place[block(c), :] = hot(iota((BLK, ROWS), 0) + c * BLK == spots)
 
+    def unbundle(w, in_ref, i, chosen, all_ref, gather, earlier=None):
+        wait_blocks(HALF, in_ref.at[w], block_recv.at[i + w])
+        half = BLK // 2
+        for c in range(CHUNKS):
+            low = dot(chosen[block(c), :SIDE], in_ref[w])
+            high = dot(chosen[block(c), SIDE:], in_ref[w])
+            first = low[:half] + pltpu.roll(high[:half], WAVE, 1)
+            last = pltpu.roll(low[half:], WAVE, 1) + high[half:]
+            all_ref[w, h, block(c, half), :] = beside(first, last).astype(BF)
+            gather.start(c)
+            if earlier is not None:
+                earlier.relay(c)
+
+    def relay(gather):
+        @pl.loop(0, CHUNKS)
+        def _(c):
+            gather.relay(c)
+
+    unbundle(0, there_in, 1, to_place, placed_all, gathers[1])
     spots_column = column_of(spots)
     for k in range(0, ROWS, BLK):
         from_place[k : k + BLK, :] = hot(iota((BLK, PTS), 1) == spots_column[k : k + BLK, :])
-    wait_blocks(SLOTS, there_in, block_recv.at[1])
-    for load in loads[2:5]:
-        load.wait()
-
-    def place(c):
-        placed_all[h, block(c), :] = dot(to_place[block(c), :], there_in[...]).astype(BF)
-
-    def project(c):
-        project_qkv(block(c), placed_all, wq, wk, wv, qq, keys, values)
-
-    pipelined(gathers[1], place, project)
-    attend(qq, keys, values, acc, att)
-
-    def unplace(b):
-        return dot(from_place[block(b), :], att[...])
-
-    scatter(unplace, back_out, back_in, block_send.at[2], block_recv.at[2])
+    unbundle(1, there_in, 1, to_place, placed_all, gathers[2], gathers[1])
     bucket_column = column_of(bucket)
     for k in range(0, PTS, BLK):
         from_bucket[k : k + BLK, :] = hot(iota((BLK, ROWS), 1) == bucket_column[k : k + BLK, :])
-    wait_blocks(SLOTS, back_in, block_recv.at[2])
+    relay(gathers[2])
+    for load in loads[2:5]:
+        load.wait()
+
+    @pl.loop(0, CHUNKS)
+    def _(c):
+        gathers[1].finish(c)
+        gathers[2].finish(c)
+        project_qkv(c, placed_all, wqkv, qq, keys, values)
+
+    for w in range(2):
+        attend(w, qq, keys, values, acc, att)
+
+        @pl.loop(0, CHUNKS)
+        def _(j):
+            b = turn_of(j)
+            low = dot(from_place[block(b), :], att[...])
+            high = dot(from_place[block(b + CHUNKS), :], att[...])
+            back_out[w, block(b), :] = beside(low[:, :W], high[:, W:]).astype(BF)
+            send_wave(w, b, back_out, back_in, 3)
+
+        keep_own(w, back_out, back_in)
+
+    unbundle(0, back_in, 3, from_bucket, merged_all, gathers[3])
+    relay(gathers[3])
+    unbundle(1, back_in, 3, from_bucket, merged_all, gathers[4])
+    relay(gathers[4])
     for load in loads[5:]:
         load.wait()
 
-    def unpack(c):
-        merged_all[h, block(c), :] = dot(from_bucket[block(c), :], back_in[...]).astype(BF)
-
     def store(c):
-        return pltpu.make_async_copy(
-            result.at[block(c)], out_hbm.at[block(c)], store_sem.at[c]
-        )
-
-    def perceive(c):
-        mlp_block(c, merged_all, h1, wp, n2_ref, f1, f2, result)
-        store(c).start()
-
-    pipelined(gathers[2], unpack, perceive)
+        rows = block(c, 2 * BLK)
+        return pltpu.make_async_copy(result.at[rows], out_hbm.at[rows], store_sem.at[c])
+
+    @pl.loop(0, CHUNKS, step=2)
+    def _(c):
+        for k in range(2):
+            gathers[3].finish(c + k)
+            gathers[4].finish(c + k)
+        mlp_blocks([c, c + 1], merged_all, h1, wp, n2_ref, f1, f2, result)
+        store(c // 2).start()
 
     for halo in halos:
         halo.wait_send()
-    for i, (size, ref) in enumerate(((NOTE, note_out), (SLOTS, there_out), (SLOTS, back_out))):
-        wait_blocks(size, ref, block_send.at[i])
+    wait_blocks(NOTE, note_out, block_send.at[0])
+    for w in range(2):
+        wait_blocks(HALF, there_out.at[w], block_send.at[1 + w])
+        wait_blocks(HALF, back_out.at[w], block_send.at[3 + w])
     for gather in gathers:
         gather.drain()
-
-    @pl.loop(0, CHUNKS)
-    def _(c):
+    for c in range(2):
         store(c).wait()
 
 
@@ -522,25 +617,23 @@
         scratch_shapes=[
             pltpu.VMEM((PTS + 2 * REACH, C), BF),
             pltpu.VMEM((TAPS, C, W), BF),
-            pltpu.VMEM((C, W), BF),
-            pltpu.VMEM((C, W), BF),
-            pltpu.VMEM((C, W), BF),
+            pltpu.VMEM((C, 3 * W), BF),
             pltpu.VMEM((C, C), BF),
             pltpu.VMEM((C, MLP), BF),
             pltpu.VMEM((MLP, C), BF),
             pltpu.VMEM((MID + 1, PTS + REACH, W), BF),
             pltpu.VMEM((MID, PTS + REACH, W), BF),
             pltpu.VMEM((HEADS, PTS, W), BF),
-            pltpu.VMEM((HEADS, PTS, W), BF),
-            pltpu.VMEM((HEADS, PTS, W), BF),
+            pltpu.VMEM((2, HEADS, PTS // 2, W), BF),
+            pltpu.VMEM((2, HEADS, PTS // 2, W), BF),
             pltpu.VMEM((PTS, C), F32),
             pltpu.VMEM((HEADS, PTS, W), BF),
             pltpu.VMEM((DEVS * NOTE, W), BF),
             pltpu.VMEM((DEVS * NOTE, W), BF),
-            pltpu.VMEM((ROWS, W), BF),
-            pltpu.VMEM((ROWS, W), BF),
-            pltpu.VMEM((ROWS, W), BF),
-            pltpu.VMEM((ROWS, W), BF),
+            pltpu.VMEM((2, SIDE, W), BF),
+            pltpu.VMEM((2, SIDE, W), BF),
+            pltpu.VMEM((2, SIDE, W), BF),
+            pltpu.VMEM((2, SIDE, W), BF),
             pltpu.VMEM((PTS, ROWS), BF),
             pltpu.VMEM((ROWS, PTS), BF),
             pltpu.VMEM((PTS, ROWS), BF),
@@ -548,16 +641,16 @@
             pltpu.VMEM((PTS, W), BF),
             pltpu.VMEM((PTS, W), BF),
             pltpu.VMEM((PTS, 2 * W), F32),
-            pltpu.VMEM((PTS, W), BF),
+            pltpu.VMEM((PTS, 2 * W), BF),
             pltpu.VMEM((PTS, C), BF),
             dma((8,)),
             dma((2,)),
             dma((2,)),
-            dma((3,)),
-            dma((3,)),
-            dma((3, 6, CHUNKS)),
-            dma((3, 6, CHUNKS)),
-            dma((CHUNKS,)),
+            dma((5,)),
+            dma((5,)),
+            dma((5, 6, CHUNKS)),
+            dma((5, 6, CHUNKS)),
+            dma((2,)),
         ],
         compiler_params=pltpu.CompilerParams(
             collective_id=0, has_side_effects=True, vmem_limit_bytes=58 * 2**20

time: 120 us -> 100 us (0.83); the launches traced: 118 us -> 100 us
  Pallas kernels: 116 us -> 97.7 us
    pallas_call x1, Pallas kernels: 116 us -> 97.7 us  [per_device(): pl.pallas_call(whole_kernel, out_shape=jax.ShapeDtypeStruct((PTS, C), BF)...]
where the time goes in v3:
time: 100 us
  Pallas kernels  97.7 us (98%)
  local copies, waits for them, and re-layouts  2.26 us (2%)
    pallas_call x1, Pallas kernels, per_device(): pl.pallas_call(whole_kernel, out_shape=jax.ShapeDtypeStruct((PTS, C), BF)...  97.7 us
    unnamed x1, local copies, waits for them, and re-layouts  2.26 us

profile of v3, /device:TPU:1, one launch (start us, length us, event | category | flops | bytes accessed | tf_op | source)
XLA Modules:
  0.0 100.0 jit_solution(15081031254690649015)
XLA Ops:
  0.0 97.7 %shard_map.127 = bf16[1024,512]{1,0:T(8,128)(2,1)} custom-call(bf16[1024,512]{1,0:T(8,128)(2,1)} %feats_hbm.1, s32[27,1024]{1,0:T(8,128)} %bitcast.5, s32[1,1024]{1,0:T(1,128)} %bitcast.6, bf16[27,512,128]{2,1,0:T(8,128)(2,1)} %cw_hbm.1, f32[1,512]{1,0:T(1,128)} %bitcast.7, f32[1,512]{1,0:T(1,128)} %bitcast.8, bf16[512,128]{1,0:T(8,128)(2,1)} %wq_hbm.1, ...), custom_call_target="tpu_custom_call" | custom-call | tf_op jit(solution)/shard_map/pallas_call | solution.py:612
  97.7 2.3 %copy.15 = bf16[1024,512]{1,0:T(8,128)(2,1)} copy(bf16[1024,512]{1,0:T(8,128)(2,1)} %shard_map.127) | data formatting | bytes 2097152

commit v4 on v3

--- a/solution.py
+++ b/solution.py
@@ -69,14 +69,14 @@
             barrier, inc=1, device_id=(lax.rem(p + k, DEVS), h), device_id_type=MESH
         )
 
-    for k in (1, HEADS - 1):
+    for k in range(1, HEADS):
         pl.semaphore_signal(
             barrier, inc=1, device_id=(p, lax.rem(h + k, HEADS)), device_id_type=MESH
         )
 
 
 def barrier_wait():
-    pl.semaphore_wait(pltpu.get_barrier_semaphore(), DEVS + 1)
+    pl.semaphore_wait(pltpu.get_barrier_semaphore(), DEVS - 1 + HEADS - 1)
 
 
 def send_block(p, h, d, size, out_ref, in_ref, send_sem, recv_sem):
@@ -98,48 +98,32 @@
 class Gather:
     def __init__(self, p, h, ref, send_sem, recv_sem):
         self.p, self.h, self.ref, self.send_sem, self.recv_sem = p, h, ref, send_sem, recv_sem
-        self.right, self.left = lax.rem(h + 1, HEADS), lax.rem(h + 3, HEADS)
-        self.half = ref.shape[1] // CHUNKS // 2
-
-    def copy(self, kind, c):
-        owner, upper, to = (
-            (self.h, True, self.right),
-            (self.h, False, self.left),
-            (self.h, False, self.right),
-            (self.h, True, self.left),
-            (self.left, True, self.right),
-            (self.right, False, self.left),
-        )[kind]
-        start = pl.multiple_of((2 * c + (0 if upper else 1)) * self.half, self.half)
-        rows = self.ref.at[owner, pl.ds(start, self.half)]
+        self.size = ref.shape[1] // CHUNKS
+
+    def copy(self, step, c, owner):
+        rows = self.ref.at[owner, block(c, self.size)]
         return pltpu.make_async_remote_copy(
             src_ref=rows,
             dst_ref=rows,
-            send_sem=self.send_sem.at[kind, c],
-            recv_sem=self.recv_sem.at[kind, c],
-            device_id=(self.p, to),
+            send_sem=self.send_sem.at[step - 1, c],
+            recv_sem=self.recv_sem.at[step - 1, c],
+            device_id=(self.p, lax.rem(self.h + step, HEADS)),
             device_id_type=MESH,
         )
 
     def start(self, c):
-        for kind in range(4):
-            self.copy(kind, c).start()
-
-    def relay(self, c):
-        self.copy(0, c).wait_recv()
-        self.copy(4, c).start()
-        self.copy(1, c).wait_recv()
-        self.copy(5, c).start()
+        for step in (2, 1, 3):
+            self.copy(step, c, self.h).start()
 
     def finish(self, c):
-        for kind in (2, 3, 4, 5):
-            self.copy(kind, c).wait_recv()
+        for step in (1, 3, 2):
+            self.copy(step, c, lax.rem(self.h + HEADS - step, HEADS)).wait_recv()
 
     def drain(self):
         @pl.loop(0, CHUNKS)
         def _(c):
-            for kind in range(6):
-                self.copy(kind, c).wait_send()
+            for step in (1, 2, 3):
+                self.copy(step, c, self.h).wait_send()
 
 
 def conv_project(ext_ref, ext_rows, y_rows, w_ref, first, count, y_ref):
@@ -268,7 +252,7 @@
     @pl.loop(wave * heads, wave * heads + heads, step=2)
     def _(first):
         pairs = [operands(first), operands(first + 1)]
-        steps = [(pair, slice(b * BLK, b * BLK + BLK)) for pair in pairs for b in range(CHUNKS)]
+        steps = [(pair, slice(b, b + BLK)) for pair in pairs for b in range(0, PTS, BLK)]
         coming = dot_nt(qq_ref[steps[0][1], :], steps[0][0][0])
         for i, ((_, values), rows) in enumerate(steps):
             scores = coming
@@ -298,23 +282,29 @@
     return h2, jnp.concatenate([part.astype(BF) for part in parts], 1)
 
 
-def mlp_blocks(chunks, att_ref, h1_ref, wp_ref, n2_ref, f1_ref, f2_ref, out_ref):
+def mlp_blocks(finish, done, att_ref, h1_ref, wp_ref, n2_ref, f1_ref, f2_ref, out_ref):
     width = C // 2
-    steps = [(i, slice(j, j + width)) for i in range(len(chunks)) for j in range(0, MLP, width)]
-    ready = [mlp_rows(chunks[0], att_ref, h1_ref, wp_ref, n2_ref)]
-    total = [ready[0][0]]
+    steps = [(i, slice(j, j + width)) for i in range(CHUNKS) for j in range(0, MLP, width)]
+    ready, total = [], []
+
+    def prepare(c):
+        finish(c)
+        ready.append(mlp_rows(c, att_ref, h1_ref, wp_ref, n2_ref))
+        total.append(ready[-1][0])
+
+    prepare(0)
     coming = dot(ready[0][1], f1_ref[:, steps[0][1]])
     for n, (i, cols) in enumerate(steps):
         x = coming
         if n + 3 < len(steps) and steps[n + 3][0] == len(ready):
-            ready.append(mlp_rows(chunks[len(ready)], att_ref, h1_ref, wp_ref, n2_ref))
-            total.append(ready[-1][0])
+            prepare(len(ready))
         if n + 1 < len(steps):
             later, ahead = steps[n + 1]
             coming = dot(ready[later][1], f1_ref[:, ahead])
         total[i] += dot(gelu(x).astype(BF), f2_ref[cols, :])
         if cols.stop == MLP:
-            out_ref[block(chunks[i]), :] = total[i].astype(BF)
+            out_ref[block(i), :] = total[i].astype(BF)
+            done(i)
 
 
 def whole_kernel(
@@ -437,8 +427,7 @@
     for halo in halos:
         halo.wait_recv()
 
-    @pl.loop(1, DEVS)
-    def _(k):
+    for k in range(1, DEVS):
         d = lax.rem(p + k, DEVS)
         send_block(p, h, d, NOTE, note_out, note_in, block_send.at[0], block_recv.at[0])
 
@@ -447,16 +436,17 @@
     conv_project(ext, pl.ds(0, REACH), pl.ds(0, REACH), cw, 0, MID, yb)
     after = pl.ds(PTS + REACH, REACH)
     conv_project(ext, after, pl.ds(PTS, REACH), cw, MID + 1, MID, yf)
-    gather.relay(1)
-    gather.relay(2)
 
     @pl.loop(0, 2)
     def _(j):
         convolve(3 * j)
         norm(1 + j)
 
-    gather.relay(0)
-    gather.relay(3)
+
+    @pl.loop(0, ROWS // BLK)
+    def _(b):
+        from_place[block(b), :] = hot(iota((BLK, PTS), 0) + b * BLK == bucket)
+
     norm(0)
     norm(3)
 
@@ -489,19 +479,18 @@
     own = normed[h]
     own = jnp.concatenate([own, turned(own)], 1)
 
+    def both_halves(b, right):
+        left = jnp.concatenate([from_place[block(b), :], from_place[block(b + CHUNKS), :]], 0)
+        product = dot(left, right)
+        return product[:BLK], product[BLK:]
+
     @pl.loop(0, CHUNKS)
     def _(j):
         b = turn_of(j)
-        row = iota((BLK, PTS), 0) + b * BLK
-        low = dot(hot(row == bucket), own)
-        high = dot(hot(row + SIDE == bucket), own)
+        low, high = both_halves(b, own)
         there_out[0, block(b), :] = beside(low[:, :W], high[:, W:]).astype(BF)
         there_out[1, block(b), :] = beside(low[:, W:], high[:, :W]).astype(BF)
         send_wave(0, b, there_out, there_in, 1)
-
-    @pl.loop(0, CHUNKS)
-    def _(j):
-        send_wave(1, turn_of(j), there_out, there_in, 1)
 
     for w in range(2):
         keep_own(w, there_out, there_in)
@@ -512,7 +501,11 @@
     def _(c):
         to_place[block(c), :] = hot(iota((BLK, ROWS), 0) + c * BLK == spots)
 
-    def unbundle(w, in_ref, i, chosen, all_ref, gather, earlier=None):
+    @pl.loop(0, CHUNKS)
+    def _(j):
+        send_wave(1, turn_of(j), there_out, there_in, 1)
+
+    def unbundle(w, in_ref, i, chosen, all_ref, gather):
         wait_blocks(HALF, in_ref.at[w], block_recv.at[i + w])
         half = BLK // 2
         for c in range(CHUNKS):
@@ -522,23 +515,15 @@
             last = pltpu.roll(low[half:], WAVE, 1) + high[half:]
             all_ref[w, h, block(c, half), :] = beside(first, last).astype(BF)
             gather.start(c)
-            if earlier is not None:
-                earlier.relay(c)
-
-    def relay(gather):
-        @pl.loop(0, CHUNKS)
-        def _(c):
-            gather.relay(c)
 
     unbundle(0, there_in, 1, to_place, placed_all, gathers[1])
     spots_column = column_of(spots)
     for k in range(0, ROWS, BLK):
         from_place[k : k + BLK, :] = hot(iota((BLK, PTS), 1) == spots_column[k : k + BLK, :])
-    unbundle(1, there_in, 1, to_place, placed_all, gathers[2], gathers[1])
+    unbundle(1, there_in, 1, to_place, placed_all, gathers[2])
     bucket_column = column_of(bucket)
     for k in range(0, PTS, BLK):
         from_bucket[k : k + BLK, :] = hot(iota((BLK, ROWS), 1) == bucket_column[k : k + BLK, :])
-    relay(gathers[2])
     for load in loads[2:5]:
         load.wait()
 
@@ -554,31 +539,30 @@
         @pl.loop(0, CHUNKS)
         def _(j):
             b = turn_of(j)
-            low = dot(from_place[block(b), :], att[...])
-            high = dot(from_place[block(b + CHUNKS), :], att[...])
+            low, high = both_halves(b, att[...])
             back_out[w, block(b), :] = beside(low[:, :W], high[:, W:]).astype(BF)
             send_wave(w, b, back_out, back_in, 3)
 
         keep_own(w, back_out, back_in)
 
     unbundle(0, back_in, 3, from_bucket, merged_all, gathers[3])
-    relay(gathers[3])
     unbundle(1, back_in, 3, from_bucket, merged_all, gathers[4])
-    relay(gathers[4])
     for load in loads[5:]:
         load.wait()
 
     def store(c):
-        rows = block(c, 2 * BLK)
-        return pltpu.make_async_copy(result.at[rows], out_hbm.at[rows], store_sem.at[c])
-
-    @pl.loop(0, CHUNKS, step=2)
-    def _(c):
-        for k in range(2):
-            gathers[3].finish(c + k)
-            gathers[4].finish(c + k)
-        mlp_blocks([c, c + 1], merged_all, h1, wp, n2_ref, f1, f2, result)
-        store(c // 2).start()
+        return pltpu.make_async_copy(
+            result.at[block(c)], out_hbm.at[block(c)], store_sem.at[c]
+        )
+
+    def merged_there(c):
+        gathers[3].finish(c)
+        gathers[4].finish(c)
+
+    mlp_blocks(
+        merged_there, lambda c: store(c).start(),
+        merged_all, h1, wp, n2_ref, f1, f2, result,
+    )
 
     for halo in halos:
         halo.wait_send()
@@ -588,7 +572,7 @@
         wait_blocks(HALF, back_out.at[w], block_send.at[3 + w])
     for gather in gathers:
         gather.drain()
-    for c in range(2):
+    for c in range(CHUNKS):
         store(c).wait()
 
 
@@ -648,9 +632,9 @@
             dma((2,)),
             dma((5,)),
             dma((5,)),
-            dma((5, 6, CHUNKS)),
-            dma((5, 6, CHUNKS)),
-            dma((2,)),
+            dma((5, 3, CHUNKS)),
+            dma((5, 3, CHUNKS)),
+            dma((CHUNKS,)),
         ],
         compiler_params=pltpu.CompilerParams(
             collective_id=0, has_side_effects=True, vmem_limit_bytes=58 * 2**20

time: 100 us -> 95.5 us (0.955)
  Pallas kernels: 97.7 us -> 92.5 us
    pallas_call x1, Pallas kernels: 97.7 us -> 92.5 us  [per_device(): pl.pallas_call(whole_kernel, out_shape=jax.ShapeDtypeStruct((PTS, C), BF)...]
where the time goes in v4:
time: 95.5 us; the launch traced here: 94.8 us
  Pallas kernels  92.5 us (97%)
  local copies, waits for them, and re-layouts  2.26 us (2%)
    pallas_call x1, Pallas kernels, per_device(): pl.pallas_call(whole_kernel, out_shape=jax.ShapeDtypeStruct((PTS, C), BF)...  92.5 us
    unnamed x1, local copies, waits for them, and re-layouts  2.26 us

profile of v4, /device:TPU:1, one launch (start us, length us, event | category | flops | bytes accessed | tf_op | source)
XLA Modules:
  0.0 94.8 jit_solution(2376468778348523325)
XLA Ops:
  0.0 92.5 %shard_map.127 = bf16[1024,512]{1,0:T(8,128)(2,1)} custom-call(bf16[1024,512]{1,0:T(8,128)(2,1)} %feats_hbm.1, s32[27,1024]{1,0:T(8,128)} %bitcast.5, s32[1,1024]{1,0:T(1,128)} %bitcast.6, bf16[27,512,128]{2,1,0:T(8,128)(2,1)} %cw_hbm.1, f32[1,512]{1,0:T(1,128)} %bitcast.7, f32[1,512]{1,0:T(1,128)} %bitcast.8, bf16[512,128]{1,0:T(8,128)(2,1)} %wq_hbm.1, ...), custom_call_target="tpu_custom_call" | custom-call | tf_op jit(solution)/shard_map/pallas_call | solution.py:596
  92.5 2.3 %copy.15 = bf16[1024,512]{1,0:T(8,128)(2,1)} copy(bf16[1024,512]{1,0:T(8,128)(2,1)} %shard_map.127) | data formatting | bytes 2097152
